TPU v7x, 128 devices: a whole 4x4x4 slice. The times are simulated.
128 devices in a mesh: dp: 8 (over y, core), group: 16 (over x, z).
Axes of the slice: x: 4, y: 4, z: 4, core: 2. Of those that a mesh axis runs over, the one named last changes fastest.
Arguments:
- tile_maps: bfloat16 [1024, 16, 16, 384], P(('dp', 'group')), may hold values from -45 to 45
- positions: int32 [2, 1024], P(None, ('dp', 'group')), may hold values from 0 to 511
- counts: int32 [8], P('dp'), may hold values from 1 to 128, as said below
- routing: int32 [8, 16, 8], P(None, 'group'), may hold values from -1 to 31, as said below
- depth_kernel: float32 [49, 384], replicated, may hold values from -0.875 to 0.875
- depth_bias: float32 [384], replicated, may hold values from -3 to 3
- norm_gain: float32 [384], replicated, may hold values from 0.25 to 1.75
- norm_shift: float32 [384], replicated, may hold values from -2 to 2
- expand_weight: bfloat16 [384, 1536], replicated, may hold values from -0.3125 to 0.3125
- expand_bias: float32 [1536], replicated, may hold values from -1.15 to -0.75
- reduce_weight: bfloat16 [1536, 384], replicated, may hold values from -0.15625 to 0.15625
- reduce_bias: float32 [384], replicated, may hold values from -2 to 2
- layer_scale: float32 [384], replicated, may hold values from 0.3 to 1.5
- head_weight: bfloat16 [384, 768], replicated, may hold values from -0.3125 to 0.3125
- slide_taps: float32 [7, 768], replicated, may hold values from -2.5 to 2.5
- slide_weight: bfloat16 [768, 768], replicated, may hold values from -0.21875 to 0.21875
- slide_bias: float32 [768], replicated, may hold values from -2 to 2
- cotangent: float32 [8, 768], P('dp'), may hold values from -180 to 180
Outputs:
- tile_out: bfloat16 [512, 16, 16, 384], P(('dp', 'group'))
- slide_feature: float32 [8, 768], P('dp')
- grad_expand: float32 [589824], P(('dp', 'group'))
- grad_reduce: float32 [589824], P(('dp', 'group'))
- grad_depth: float32 [18816], P(('dp', 'group'))
Inputs may be any that keep to these rules, and one draw needn't show every extreme that they name: counts[d] is the number of tiles of slide d. At each group index the present tiles of all slides number at most 32, at group index 0 exactly that. routing[d, g, s] is -1 where the slot holds no tile, else e * 4 + p: the tile is processed at slot p of the device with dp index e and group index g. Each processing slot receives at most one tile; at group index 0 every one receives a tile. A device sends at most 1 tiles to each dp index, and some device sends exactly 1 to each.
All inputs are finite; a program needn't handle non-finite values.
Results may differ from a plain program's by a relative error of at most 0.013.
Values may be sent and summed in bfloat16 or wider, within the bound.
A program may use at most 128 MiB of HBM per device.

v0:
```python
import math

import jax
import jax.numpy as jnp
from jax import lax
from jax.sharding import PartitionSpec as P

E = 768
KS = 7
KERNEL_TAPS = 7
TILE_DILATION = 3
PROC = 4


EPSILON = 1e-06
HALF_ROOT = 0.7071067811865476
INV_ROOT_TAU = 0.3989422804014327


def gelu_exact(values):
    return 0.5 * values * (1.0 + jax.scipy.special.erf(values * HALF_ROOT))


def gelu_slope(values):
    return 0.5 * (
        1.0 + jax.scipy.special.erf(values * HALF_ROOT)
    ) + values * INV_ROOT_TAU * jnp.exp(-0.5 * values * values)


def contract_rows(left_side, right_side):
    return lax.dot_general(
        left_side, right_side, (((0,), (0,)), ((), ())), preferred_element_type=jnp.float32
    )


def contract_cols(left_side, right_side):
    return lax.dot_general(
        left_side, right_side, (((1,), (1,)), ((), ())), preferred_element_type=jnp.float32
    )


def padded_tiles(work_tiles):
    border_width = KS // 2
    return jnp.pad(
        work_tiles, ((0, 0), (border_width, border_width), (border_width, border_width), (0, 0))
    )


def block_forward(
    work_tiles,
    depth_kernel,
    depth_bias,
    norm_gain,
    norm_shift,
    expand_weight,
    expand_bias,
    reduce_weight,
    reduce_bias,
    layer_scale,
    head_weight,
):
    tile_count = work_tiles.shape[0]
    tile_side = work_tiles.shape[1]
    channels = work_tiles.shape[3]
    pixels = tile_side * tile_side
    padded = padded_tiles(work_tiles)
    running = jnp.zeros(work_tiles.shape, jnp.float32) + depth_bias
    for tap_row in range(KS):
        for tap_col in range(KS):
            running = (
                running
                + depth_kernel[tap_row * KS + tap_col]
                * padded[:, tap_row : tap_row + tile_side, tap_col : tap_col + tile_side]
            )
    depth_out = running.reshape(tile_count * pixels, channels)
    chan_mean = jnp.mean(depth_out, axis=1, keepdims=True)
    centred = depth_out - chan_mean
    inv_std = lax.rsqrt(jnp.mean(centred * centred, axis=1, keepdims=True) + EPSILON)
    unit_norm = centred * inv_std
    normed = (unit_norm * norm_gain + norm_shift).astype(jnp.bfloat16)
    pre_act = jnp.dot(normed, expand_weight, preferred_element_type=jnp.float32) + expand_bias
    hidden = gelu_exact(pre_act).astype(jnp.bfloat16)
    mlp_out = jnp.dot(hidden, reduce_weight, preferred_element_type=jnp.float32) + reduce_bias
    section_rows = (
        work_tiles.reshape(tile_count * pixels, channels) + layer_scale * mlp_out
    ).astype(jnp.bfloat16)
    head_pre = jnp.dot(section_rows, head_weight, preferred_element_type=jnp.float32)
    tile_embed = jnp.mean(gelu_exact(head_pre).reshape(tile_count, pixels, -1), axis=1).astype(
        jnp.bfloat16
    )
    return (
        section_rows.reshape(work_tiles.shape),
        tile_embed,
        (unit_norm, inv_std, normed, pre_act, hidden, head_pre),
    )


def block_backward(
    work_tiles,
    saved_acts,
    embed_grad,
    norm_gain,
    expand_weight,
    reduce_weight,
    layer_scale,
    head_weight,
):
    unit_norm, inv_std, normed, pre_act, hidden, head_pre = saved_acts
    tile_count = work_tiles.shape[0]
    tile_side = work_tiles.shape[1]
    channels = work_tiles.shape[3]
    pixels = tile_side * tile_side
    slope_head = gelu_slope(head_pre).reshape(tile_count, pixels, -1)
    grad_head = (embed_grad.astype(jnp.float32)[:, None, :] / float(pixels) * slope_head).astype(
        jnp.bfloat16
    )
    grad_head = grad_head.reshape(tile_count * pixels, -1)
    grad_block = contract_cols(grad_head, head_weight)
    grad_mlp = (layer_scale * grad_block).astype(jnp.bfloat16)
    reduce_grad = contract_rows(hidden, grad_mlp)
    grad_hidden = contract_cols(grad_mlp, reduce_weight)
    grad_pre = (grad_hidden * gelu_slope(pre_act)).astype(jnp.bfloat16)
    expand_grad = contract_rows(normed, grad_pre)
    grad_norm = contract_cols(grad_pre, expand_weight)
    scaled_grad = grad_norm * norm_gain
    grad_depthwise = inv_std * (
        scaled_grad
        - jnp.mean(scaled_grad, axis=1, keepdims=True)
        - unit_norm * jnp.mean(scaled_grad * unit_norm, axis=1, keepdims=True)
    )
    grad_depthwise = grad_depthwise.reshape(tile_count, tile_side, tile_side, channels)
    padded = padded_tiles(work_tiles)
    tap_grads = []
    for tap_row in range(KS):
        for tap_col in range(KS):
            tap_grads.append(
                jnp.sum(
                    grad_depthwise
                    * padded[:, tap_row : tap_row + tile_side, tap_col : tap_col + tile_side],
                    axis=(0, 1, 2),
                )
            )
    return (expand_grad, reduce_grad, jnp.stack(tap_grads))


def position_code(positions):
    half_width = E // 2
    channel_ids = jnp.arange(half_width, dtype=jnp.int32)
    frequency = jnp.exp(
        (2 * (channel_ids // 2)).astype(jnp.float32) * (-math.log(10000.0) / half_width)
    )
    pieces = []
    for coord_axis in range(2):
        angles = positions[coord_axis].astype(jnp.float32)[:, None] * frequency[None, :]
        pieces.append(jnp.where(channel_ids % 2 == 0, jnp.sin(angles), jnp.cos(angles)))
    return jnp.concatenate(pieces, axis=1)


def dilate(seq_float, slide_taps, travel_direction):
    length = seq_float.shape[0]
    border_width = KERNEL_TAPS // 2 * TILE_DILATION
    padded = jnp.pad(seq_float, ((border_width, border_width), (0, 0)))
    running = jnp.zeros(seq_float.shape, jnp.float32)
    for shift_amount in range(KERNEL_TAPS):
        leading_row = (
            border_width + travel_direction * (shift_amount - KERNEL_TAPS // 2) * TILE_DILATION
        )
        running = running + slide_taps[shift_amount] * padded[leading_row : leading_row + length]
    return running


def slide_pass(sequence, seq_present, slide_count, slide_cot, slide_taps, slide_weight, slide_bias):
    seq_float = sequence.astype(jnp.float32)
    mixed = (seq_float + dilate(seq_float, slide_taps, 1)).astype(jnp.bfloat16)
    agg_pre = jnp.dot(mixed, slide_weight, preferred_element_type=jnp.float32) + slide_bias
    weight = seq_present.astype(jnp.float32) / slide_count.astype(jnp.float32)
    feature = jnp.sum(gelu_exact(agg_pre) * weight[:, None], axis=0)
    grad_agg = (slide_cot[None, :] * weight[:, None] * gelu_slope(agg_pre)).astype(jnp.bfloat16)
    grad_mixed = contract_cols(grad_agg, slide_weight)
    seq_grad = (
        (grad_mixed + dilate(grad_mixed, slide_taps, -1)) * seq_present.astype(jnp.float32)[:, None]
    ).astype(jnp.bfloat16)
    return (feature, seq_grad)


def sender_table(my_list, slides, places):
    dest_dev = jnp.where(my_list >= 0, my_list // PROC, -1)
    is_hit = dest_dev[None, :] == jnp.arange(slides, dtype=jnp.int32)[:, None]
    order_rank = jnp.cumsum(is_hit.astype(jnp.int32), axis=1) - 1
    chosen = is_hit[:, None, :] & (
        order_rank[:, None, :] == jnp.arange(places, dtype=jnp.int32)[None, :, None]
    )
    return chosen.reshape(slides * places, -1)


def receiver_table(route_rows, my_slide, places):
    dest_dev = jnp.where(route_rows >= 0, route_rows // PROC, -1)
    is_hit = dest_dev == my_slide
    order_rank = jnp.cumsum(is_hit.astype(jnp.int32), axis=1) - 1
    chosen = is_hit[:, None, :] & (
        order_rank[:, None, :] == jnp.arange(places, dtype=jnp.int32)[None, :, None]
    )
    target = jnp.sum(jnp.where(chosen, (route_rows % PROC)[:, None, :], 0), axis=2).reshape(-1)
    is_used = jnp.any(chosen, axis=2).reshape(-1)
    return (target[None, :] == jnp.arange(PROC, dtype=jnp.int32)[:, None]) & is_used[None, :]


def on_device(
    tile_maps,
    positions,
    counts,
    routing,
    depth_kernel,
    depth_bias,
    norm_gain,
    norm_shift,
    expand_weight,
    expand_bias,
    reduce_weight,
    reduce_bias,
    layer_scale,
    head_weight,
    slide_taps,
    slide_weight,
    slide_bias,
    cotangent,
):
    params = (
        depth_kernel,
        depth_bias,
        norm_gain,
        norm_shift,
        expand_weight,
        expand_bias,
        reduce_weight,
        reduce_bias,
        layer_scale,
        head_weight,
    )
    slides = lax.axis_size("dp")
    members = lax.axis_size("group")
    my_slide = lax.axis_index("dp")
    my_member = lax.axis_index("group")
    slot_count = tile_maps.shape[0]
    embed_width = head_weight.shape[1]
    places = slot_count // slides
    route_rows = routing[:, 0, :]
    my_list = lax.dynamic_index_in_dim(route_rows, my_slide, 0, keepdims=False)
    send_pick = sender_table(my_list, slides, places).astype(jnp.bfloat16)
    take_bool = receiver_table(route_rows, my_slide, places)
    take_pick = take_bool.astype(jnp.bfloat16)
    filled = jnp.any(take_bool, axis=1)
    packed = jnp.dot(
        send_pick, tile_maps.reshape(slot_count, -1), preferred_element_type=jnp.float32
    ).astype(jnp.bfloat16)
    packed = packed.reshape((slides * places,) + tile_maps.shape[1:])
    arrived = lax.all_to_all(packed, "dp", split_axis=0, concat_axis=0, tiled=True)
    work_tiles = jnp.dot(
        take_pick, arrived.reshape(slides * places, -1), preferred_element_type=jnp.float32
    ).astype(jnp.bfloat16)
    work_tiles = work_tiles.reshape((take_pick.shape[0],) + tile_maps.shape[1:])
    section_out, tile_embed, saved_acts = block_forward(work_tiles, *params)
    tile_out = jnp.where(filled[:, None, None, None], section_out, jnp.zeros((), jnp.bfloat16))
    returned = contract_rows(take_pick, tile_embed).astype(jnp.bfloat16)
    came_back = lax.all_to_all(returned, "dp", split_axis=0, concat_axis=0, tiled=True)
    own_emb = contract_rows(send_pick, came_back)
    slide_count = counts[0]
    own_seq = jnp.arange(slot_count, dtype=jnp.int32) * members + my_member
    own_present = own_seq < slide_count
    slide_rows = jnp.where(
        own_present[:, None],
        (own_emb + position_code(positions)).astype(jnp.bfloat16),
        jnp.zeros((), jnp.bfloat16),
    )
    gathered = lax.all_gather(
        slide_rows.reshape(slot_count, 1, embed_width), "group", axis=1, tiled=True
    )
    sequence = gathered.reshape(slot_count * members, embed_width)
    seq_present = jnp.arange(slot_count * members, dtype=jnp.int32) < slide_count
    slide_cot = cotangent[0]
    feature, seq_grad = slide_pass(
        sequence, seq_present, slide_count, slide_cot, slide_taps, slide_weight, slide_bias
    )
    own_grad = lax.dynamic_index_in_dim(
        seq_grad.reshape(slot_count, members, embed_width), my_member, 1, keepdims=False
    )
    outgoing = jnp.dot(send_pick, own_grad, preferred_element_type=jnp.float32).astype(jnp.bfloat16)
    incoming = lax.all_to_all(outgoing, "dp", split_axis=0, concat_axis=0, tiled=True)
    embed_grad = jnp.dot(take_pick, incoming, preferred_element_type=jnp.float32).astype(
        jnp.bfloat16
    )
    source_tiles, _ = lax.optimization_barrier((work_tiles, embed_grad))
    kept_acts = block_forward(source_tiles, *params)[2]
    expand_grad, reduce_grad, depth_grad = block_backward(
        source_tiles,
        kept_acts,
        embed_grad,
        norm_gain,
        expand_weight,
        reduce_weight,
        layer_scale,
        head_weight,
    )
    shares = (
        lax.psum_scatter(expand_grad.reshape(-1), ("dp", "group"), scatter_dimension=0, tiled=True),
        lax.psum_scatter(reduce_grad.reshape(-1), ("dp", "group"), scatter_dimension=0, tiled=True),
        lax.psum_scatter(depth_grad.reshape(-1), ("dp", "group"), scatter_dimension=0, tiled=True),
    )
    return (tile_out, feature[None, :], shares[0], shares[1], shares[2])


def solution(mesh):
    return jax.shard_map(
        on_device,
        mesh=mesh,
        in_specs=(
            P(("dp", "group"), None, None, None),
            P(None, ("dp", "group")),
            P("dp"),
            P(None, "group", None),
            P(),
            P(),
            P(),
            P(),
            P(),
            P(),
            P(),
            P(),
            P(),
            P(),
            P(),
            P(),
            P(),
            P("dp", None),
        ),
        out_specs=(
            P(("dp", "group"), None, None, None),
            P("dp", None),
            P(("dp", "group")),
            P(("dp", "group")),
            P(("dp", "group")),
        ),
        check_vma=False,
    )
```

profile of v0, /device:TPU:1, one launch (start us, length us, event | category | flops | bytes accessed | tf_op | source)
XLA Modules:
  0.0 371.2 jit_solution(15879071314645622072)
XLA Ops:
  8.1 2.3 copy.39
  12.4 6.1 %all-to-all-start = ((bf16[8,16,16,384]{3,2,1,0:T(8,128)(2,1)}), bf16[8,16,16,384]{3,2,1,0:T(8,128)(2,1)S(1)}, u32[]{:S(2)}, u32[]{:S(2)}) async-start(bf16[8,16,16,384]{3,2,1,0:T(8,128)(2,1)} %copy.32), calls=%async_computation | async-start | bytes 3145728 | tf_op jit(solution)/shard_map/all_to_all | solution.py:257
  26.4 12.8 %all-to-all-done = bf16[8,16,16,384]{3,2,1,0:T(8,128)(2,1)S(1)} async-done(((bf16[8,16,16,384]{3,2,1,0:T(8,128)(2,1)}), bf16[8,16,16,384]{3,2,1,0:T(8,128)(2,1)S(1)}, u32[]{:S(2)}, u32[]{:S(2)}) %all-to-all-start) | async-done | bytes 1572896 | tf_op jit(solution)/shard_map/all_to_all | solution.py:257
  43.3 12.8 %fusion.203 = (f32[4,16,16]{2,1,0:T(8,128)S(1)}, f32[4,16,16,384]{3,2,1,0:T(8,128)S(1)}) fusion(f32[384]{0:T(512)S(1)} %copy-done.11, f32[384]{0:T(512)S(1)} %copy-done.12, f32[384]{0:T(512)S(1)} %copy-done.33, f32[384]{0:T(512)S(1)} %copy-done.34, f32[384]{0:T(512)S(1)} %copy-done.35, f32[384]{0:T(512)S(1)} %copy-done.36, f32[384]{0:T(512)S(1)} %copy-done.37, ...), kind=kLoop, calls=%fused_computation.532 | loop fusion | flops 58194944 | bytes 2440192 | tf_op jit(solution)/shard_map/reduce_sum | solution.py:76
  61.4 1.9 fusion.112
  63.4 5.5 %add_convert_fusion.1 = bf16[1024,384]{1,0:T(8,128)(2,1)S(1)} fusion(f32[1024,384]{1,0:T(8,128)} %reshape.395, bf16[1536,384]{1,0:T(8,128)(2,1)} %param.28, bf16[1024,384]{1,0:T(8,128)(2,1)} %fusion.112, bf16[384,1536]{1,0:T(8,128)(2,1)S(1)} %copy-done, f32[1536]{0:T(1024)} %param.27, f32[384]{0:T(512)} %param.29, f32[384]{0:T(512)} %param.30), kind=kOutput, calls=%fused_computation.323 | convolution fusion | flops 2426929152 | bytes 5514240 | tf_op jit(solution)/shard_map/dot_general | solution.py:83
  72.4 4.1 %all-to-all-start.1 = ((bf16[8,2,384]{2,1,0:T(2,128)(2,1)}), bf16[8,2,384]{2,1,0:T(2,128)(2,1)S(1)}, u32[]{:S(2)}, u32[]{:S(2)}) async-start(bf16[8,2,384]{2,1,0:T(2,128)(2,1)} %reshape.458), calls=%async_computation.1 | async-start | bytes 24576 | tf_op jit(solution)/shard_map/all_to_all | solution.py:265
  76.6 4.6 %all-to-all-done.1 = bf16[8,2,384]{2,1,0:T(2,128)(2,1)S(1)} async-done(((bf16[8,2,384]{2,1,0:T(2,128)(2,1)}), bf16[8,2,384]{2,1,0:T(2,128)(2,1)S(1)}, u32[]{:S(2)}, u32[]{:S(2)}) %all-to-all-start.1) | async-done | bytes 12320 | tf_op jit(solution)/shard_map/all_to_all | solution.py:265
  81.4 19.9 %all-gather = bf16[8,12288]{1,0:T(8,128)(2,1)S(1)} all-gather(bf16[8,768]{1,0:T(8,128)(2,1)S(1)} %fusion.116), channel_id=2, replica_groups=mesh['dp'=8,'group'=16] {'group'}, dimensions={1}, use_global_device_ids=true | all-gather | bytes 208896 | tf_op jit(solution)/shard_map/all_gather | solution.py:275
  101.4 2.6 multiply_reduce_fusion.4
  105.8 12.9 %all_to_all.29 = bf16[8,2,384]{2,1,0:T(2,128)(2,1)S(1)} all-to-all(bf16[8,2,384]{2,1,0:T(2,128)(2,1)S(1)} %reshape.460), channel_id=1, replica_groups=mesh['dp'=8,'group'=16] {'dp'}, dimensions={0} | all-to-all | bytes 24576 | tf_op jit(solution)/shard_map/all_to_all | solution.py:288
  119.5 13.6 %fusion.199 = (f32[4,16,16]{2,1,0:T(8,128)S(1)}, f32[4,16,16,384]{3,2,1,0:T(8,128)S(1)}) fusion(f32[384]{0:T(512)} %get-tuple-element.105, f32[384]{0:T(512)} %get-tuple-element.106, f32[384]{0:T(512)} %get-tuple-element.59, f32[384]{0:T(512)} %get-tuple-element.60, f32[384]{0:T(512)} %get-tuple-element.61, f32[384]{0:T(512)} %get-tuple-element.62, ...), kind=kLoop, calls=%fused_computation.530 | loop fusion | flops 58194944 | bytes 2440192 | tf_op jit(solution)/shard_map/reduce_sum | solution.py:76
  137.9 2.7 multiply_convert_fusion
  140.6 1.8 fusion.107
  142.5 1.8 fusion.9
  145.3 3.3 fusion.206
  148.6 3.5 fusion.4
  152.0 2.9 fusion.205
  154.9 2.0 fusion.198
  156.9 6.2 %fusion.105 = (f32[384]{0:T(512)S(1)}, f32[384]{0:T(512)}, f32[384]{0:T(512)}, f32[384]{0:T(512)}, f32[384]{0:T(512)}, /*index=5*/f32[384]{0:T(512)}, f32[384]{0...) fusion(bf16[4,16,16,384]{3,2,1,0:T(8,128)(2,1)S(1)} %bitcast.16, ...), kind=kLoop, calls=%fused_computation.306 | loop fusion | flops 23586048 | bytes 5549056 | tf_op jit(solution)/shard_map/reduce_sum | solution.py:137
  163.1 3.2 fusion.104
  166.3 4.4 %fusion.106 = (f32[384]{0:T(512)}, f32[384]{0:T(512)}, f32[384]{0:T(512)}, f32[384]{0:T(512)}, f32[384]{0:T(512)}, /*index=5*/f32[384]{0:T(512)}, f32[384]{0:T(5...) fusion(bf16[4,16,16,384]{3,2,1,0:T(8,128)(2,1)S(1)} %bitcast.16, ...), kind=kLoop, calls=%fused_computation.307 | loop fusion | flops 21226752 | bytes 2386944 | tf_op jit(solution)/shard_map/reduce_sum | solution.py:137
  170.7 3.3 reshape.391
  209.4 150.8 %all-reduce.10.cloned.1.call-done = (f32[589824]{0:T(1024)}, f32[589824]{0:T(1024)}, f32[18816]{0:T(1024)}) async-done(((f32[589824]{0:T(1024)}, f32[589824]{0:T(1024)}, f32[18816]{0:T(1024)}), (f32[589824]{0:T(1024)}, f32[589824]{0:T(1024)}, f32[18816]{0:T(1024)})) %all-reduce.10.cloned.1.call-update) | async-done | bytes 4793872
  (271 shorter events, 70.5 us)
Async XLA Ops:
  7.2 56.2 %copy-start = (bf16[384,1536]{1,0:T(8,128)(2,1)S(1)}, bf16[384,1536]{1,0:T(8,128)(2,1)}, u32[]{:S(2)}) copy-start(bf16[384,1536]{1,0:T(8,128)(2,1)} %param.26) | copy-start | bytes 3538948
  12.4 6.1 %copy-start.64 = (s32[8,1,8]{2,1,0:T(1,128)S(1)}, s32[8,1,8]{2,1,0:T(1,128)}, u32[]{:S(2)}) copy-start(s32[8,1,8]{2,1,0:T(1,128)} %param.21) | copy-start | bytes 772
  12.4 9.9 %copy-start.4 = (f32[49,384]{1,0:T(8,128)S(1)}, f32[49,384]{1,0:T(8,128)}, u32[]{:S(2)}) copy-start(f32[49,384]{1,0:T(8,128)} %param.22) | copy-start | bytes 225796
  12.4 10.5 %copy-start.5 = (f32[7,768]{1,0:T(8,128)S(1)}, f32[7,768]{1,0:T(8,128)}, u32[]{:S(2)}) copy-start(f32[7,768]{1,0:T(8,128)} %param.32) | copy-start | bytes 64516
  12.4 13.2 %copy-start.67 = (s32[2,8]{1,0:T(2,128)S(1)}, s32[2,8]{1,0:T(2,128)}, u32[]{:S(2)}) copy-start(s32[2,8]{1,0:T(2,128)} %param.19) | copy-start | bytes 196
  12.4 26.8 %all-to-all-start = ((bf16[8,16,16,384]{3,2,1,0:T(8,128)(2,1)}), bf16[8,16,16,384]{3,2,1,0:T(8,128)(2,1)S(1)}, u32[]{:S(2)}, u32[]{:S(2)}) async-start(bf16[8,16,16,384]{3,2,1,0:T(8,128)(2,1)} %copy.32), calls=%async_computation | async-start | bytes 3145728 | tf_op jit(solution)/shard_map/all_to_all | solution.py:257
  25.6 14.5 %copy-start.61 = (pred[4,8]{1,0:T(4,128)(4,1)}, pred[4,8]{1,0:T(4,128)(4,1)S(1)}, u32[]{:S(2)}) copy-start(pred[4,8]{1,0:T(4,128)(4,1)S(1)} %get-tuple-element.121) | copy-start | bytes 100
  68.9 7.6 %copy-start.65 = (f32[1,768]{1,0:T(1,128)S(1)}, f32[1,768]{1,0:T(1,128)}, u32[]{:S(2)}) copy-start(f32[1,768]{1,0:T(1,128)} %param.35) | copy-start | bytes 9220
  68.9 12.3 %copy-start.52 = (f32[8,384]{1,0:T(8,128)S(1)}, f32[8,384]{1,0:T(8,128)}, u32[]{:S(2)}) copy-start(f32[8,384]{1,0:T(8,128)} %get-tuple-element.129) | copy-start | bytes 36868
  68.9 12.3 %copy-start.53 = (f32[8,384]{1,0:T(8,128)S(1)}, f32[8,384]{1,0:T(8,128)}, u32[]{:S(2)}) copy-start(f32[8,384]{1,0:T(8,128)} %get-tuple-element.130) | copy-start | bytes 36868
  69.0 12.3 %copy-start.56 = (pred[8,8]{1,0:T(8,128)(4,1)S(1)}, pred[8,8]{1,0:T(8,128)(4,1)}, u32[]{:S(2)}) copy-start(pred[8,8]{1,0:T(8,128)(4,1)} %copy-done.55) | copy-start | bytes 196
  69.0 32.4 %copy-start.45 = (f32[768]{0:T(1024)S(1)}, f32[768]{0:T(1024)}, u32[]{:S(2)}) copy-start(f32[768]{0:T(1024)} %get-tuple-element.107) | copy-start | bytes 9220
  69.0 32.4 %copy-start.46 = (f32[768]{0:T(1024)S(1)}, f32[768]{0:T(1024)}, u32[]{:S(2)}) copy-start(f32[768]{0:T(1024)} %get-tuple-element.108) | copy-start | bytes 9220
  69.0 32.4 %copy-start.47 = (f32[768]{0:T(1024)S(1)}, f32[768]{0:T(1024)}, u32[]{:S(2)}) copy-start(f32[768]{0:T(1024)} %get-tuple-element.109) | copy-start | bytes 9220
  69.0 32.4 %copy-start.48 = (f32[768]{0:T(1024)S(1)}, f32[768]{0:T(1024)}, u32[]{:S(2)}) copy-start(f32[768]{0:T(1024)} %get-tuple-element.110) | copy-start | bytes 9220
  69.0 32.4 %copy-start.49 = (f32[768]{0:T(1024)S(1)}, f32[768]{0:T(1024)}, u32[]{:S(2)}) copy-start(f32[768]{0:T(1024)} %get-tuple-element.111) | copy-start | bytes 9220
  69.0 32.4 %copy-start.50 = (f32[768]{0:T(1024)S(1)}, f32[768]{0:T(1024)}, u32[]{:S(2)}) copy-start(f32[768]{0:T(1024)} %get-tuple-element.112) | copy-start | bytes 9220
  69.0 32.4 %copy-start.51 = (f32[768]{0:T(1024)S(1)}, f32[768]{0:T(1024)}, u32[]{:S(2)}) copy-start(f32[768]{0:T(1024)} %get-tuple-element.113) | copy-start | bytes 9220
  69.0 32.4 %copy-start.74 = (f32[768]{0:T(1024)S(1)}, f32[768]{0:T(1024)}, u32[]{:S(2)}) copy-start(f32[768]{0:T(1024)} %param.34) | copy-start | bytes 9220
  69.0 32.4 %copy-start.77 = (f32[128]{0:T(128)S(1)}, f32[128]{0:T(128)}, u32[]{:S(2)}) copy-start(f32[128]{0:T(128)} %compare_select_fusion.8) | copy-start | bytes 1540
  72.4 8.8 %all-to-all-start.1 = ((bf16[8,2,384]{2,1,0:T(2,128)(2,1)}), bf16[8,2,384]{2,1,0:T(2,128)(2,1)S(1)}, u32[]{:S(2)}, u32[]{:S(2)}) async-start(bf16[8,2,384]{2,1,0:T(2,128)(2,1)} %reshape.458), calls=%async_computation.1 | async-start | bytes 24576 | tf_op jit(solution)/shard_map/all_to_all | solution.py:265
  76.5 283.7 %all-reduce.10.cloned.1.call-start = ((), (), s32[]{:S(2)}) async-start(), calls=%async_computation.3 | async-start | bytes 9592832
  174.0 23.1 %copy-start.60 = (f32[384]{0:T(512)S(1)}, f32[384]{0:T(512)}, u32[]{:S(2)}) copy-start(f32[384]{0:T(512)} %get-tuple-element.40) | copy-start | bytes 4612
  174.0 23.1 %copy-start.59 = (f32[384]{0:T(512)S(1)}, f32[384]{0:T(512)}, u32[]{:S(2)}) copy-start(f32[384]{0:T(512)} %get-tuple-element.41) | copy-start | bytes 4612
  (57 other events, 69.1 us)
Sparse Core Ops, SparseCore 0:
  206.8 153.3 all-reduce.9
where the time goes:
time: 373 us; the launch traced here: 371 us
  waiting for transfers between devices  168 us (45%)
  local copies, waits for them, and re-layouts  57.7 us (15%)
  other arithmetic  55.4 us (15%)
  blocking collectives  32.8 us (9%)
  matrix products  31.1 us (8%)
  between operations  15.8 us (4%)
  starting transfers between devices  10.2 us (3%)
    unnamed x2, waiting for transfers between devices  151 us
    another operation x50, local copies, waits for them, and re-layouts, block_backward(): return (expand_grad, reduce_grad, jnp.stack(tap_grads))  30.5 us
    reduce_sum x2, other arithmetic, block_forward(): chan_mean = jnp.mean(depth_out, axis=1, keepdims=True)  26.4 us
    all_gather x1, blocking collectives, on_device(): lax.all_gather(slide_rows.reshape(slot_count, 1, embed_width), 'group', a...  19.9 us
    reduce_sum x3, other arithmetic, block_backward(): jnp.sum(grad_depthwise * padded[:, tap_row:tap_row + tile_side, tap_col:t...  13.8 us
    all_to_all x1, blocking collectives, on_device(): lax.all_to_all(outgoing, 'dp', split_axis=0, concat_axis=0, tiled=True)  12.9 us
    all_to_all x1, waiting for transfers between devices, on_device(): lax.all_to_all(packed, 'dp', split_axis=0, concat_axis=0, tiled=True)  12.8 us
    unnamed x166, local copies, waits for them, and re-layouts  10.3 us
  transfers between devices with their start and end apart: 3, of which 3 were waited for; matrix products, arithmetic and copies ran while one was open for 2% of the time, Pallas kernels for 0%

commit v1 on v0

--- a/solution.py
+++ b/solution.py
@@ -3,6 +3,8 @@
 import jax
 import jax.numpy as jnp
 from jax import lax
+from jax.experimental import pallas as pl
+from jax.experimental.pallas import tpu as pltpu
 from jax.sharding import PartitionSpec as P
 
 E = 768
@@ -156,52 +158,211 @@
     return jnp.concatenate(pieces, axis=1)
 
 
-def dilate(seq_float, slide_taps, travel_direction):
-    length = seq_float.shape[0]
-    border_width = KERNEL_TAPS // 2 * TILE_DILATION
-    padded = jnp.pad(seq_float, ((border_width, border_width), (0, 0)))
-    running = jnp.zeros(seq_float.shape, jnp.float32)
-    for shift_amount in range(KERNEL_TAPS):
-        leading_row = (
-            border_width + travel_direction * (shift_amount - KERNEL_TAPS // 2) * TILE_DILATION
-        )
-        running = running + slide_taps[shift_amount] * padded[leading_row : leading_row + length]
-    return running
-
-
-def slide_pass(sequence, seq_present, slide_count, slide_cot, slide_taps, slide_weight, slide_bias):
-    seq_float = sequence.astype(jnp.float32)
-    mixed = (seq_float + dilate(seq_float, slide_taps, 1)).astype(jnp.bfloat16)
-    agg_pre = jnp.dot(mixed, slide_weight, preferred_element_type=jnp.float32) + slide_bias
-    weight = seq_present.astype(jnp.float32) / slide_count.astype(jnp.float32)
-    feature = jnp.sum(gelu_exact(agg_pre) * weight[:, None], axis=0)
-    grad_agg = (slide_cot[None, :] * weight[:, None] * gelu_slope(agg_pre)).astype(jnp.bfloat16)
-    grad_mixed = contract_cols(grad_agg, slide_weight)
-    seq_grad = (
-        (grad_mixed + dilate(grad_mixed, slide_taps, -1)) * seq_present.astype(jnp.float32)[:, None]
-    ).astype(jnp.bfloat16)
-    return (feature, seq_grad)
-
-
-def sender_table(my_list, slides, places):
+MESH = pl.DeviceIdType.MESH
+PARTS = (32, 32, 16)
+ORDERS = ("yxz", "xzy", "zyx")
+ROWS = sum(PARTS)
+
+def torus_place():
+    dp, group = lax.axis_index("dp"), lax.axis_index("group")
+    return {"y": lax.div(dp, 2), "c": lax.rem(dp, 2), "x": lax.div(group, 4), "z": lax.rem(group, 4)}
+
+def torus_device(place, **moved):
+    at = {**place, **moved}
+    return (at["y"] * 2 + at["c"], at["x"] * 4 + at["z"])
+
+def reduce_scatter_kernel(grads, out, core_in, s1, s2, s3, r1, r2, r3, core_send, core_recv, send, recv):
+    place = torus_place()
+    partner = torus_device(place, c=1 - place["c"])
+    barrier = pltpu.get_barrier_semaphore()
+    pl.semaphore_signal(barrier, inc=1, device_id=partner, device_id_type=MESH)
+    for axis in "yxz":
+        for k in (1, 2, 3):
+            pl.semaphore_signal(barrier, inc=1, device_id=torus_device(place, **{axis: lax.rem(place[axis] + k, 4)}), device_id_type=MESH)
+    pl.semaphore_wait(barrier, 10)
+
+    core_copies = []
+    for y in range(4):
+        cp = pltpu.make_async_remote_copy(src_ref=grads.at[y, 1 - place["c"]], dst_ref=core_in.at[y], send_sem=core_send.at[y], recv_sem=core_recv.at[y], device_id=partner, device_id_type=MESH)
+        cp.start()
+        core_copies.append(cp)
+
+    def start(stage, part, source, landing):
+        axis = ORDERS[part][stage]
+        made = []
+        for k in (2, 1, 3):
+            to = lax.rem(place[axis] + k, 4)
+            cp = pltpu.make_async_remote_copy(src_ref=source.at[to], dst_ref=landing.at[k - 1], send_sem=send.at[stage * 9 + part * 3 + k - 1], recv_sem=recv.at[stage * 9 + part * 3 + k - 1], device_id=torus_device(place, **{axis: to}), device_id_type=MESH)
+            cp.start()
+            made.append(cp)
+        return made
+
+    f32 = jnp.float32
+    for y in range(4):
+        core_copies[y].wait_recv()
+        for x in range(4):
+            both = grads[y, place["c"], x].astype(f32) + core_in[y, x].astype(f32)
+            both = both.astype(jnp.bfloat16)
+            s1[0][y, x] = both[:, 0:32]
+            s1[1][x, :, y] = both[:, 32:64]
+            for z in range(4):
+                s1[2][z, y, x] = both[z, 64:80]
+    flying = [start(0, part, s1[part], r1[part]) for part in range(3)]
+    flying2 = []
+    for part in range(3):
+        for cp in flying[part]:
+            cp.wait_recv()
+        mine = place[ORDERS[part][0]]
+        for a in range(4):
+            total = s1[part][mine, a].astype(f32)
+            for k in range(3):
+                total = total + r1[part][k, a].astype(f32)
+            s2[part][a] = total.astype(jnp.bfloat16)
+        flying2.append(start(1, part, s2[part], r2[part]))
+    flying3 = []
+    for part in range(3):
+        for cp in flying2[part]:
+            cp.wait_recv()
+        mine = place[ORDERS[part][1]]
+        total = s2[part][mine].astype(f32)
+        for k in range(3):
+            total = total + r2[part][k].astype(f32)
+        s3[part][...] = total.astype(jnp.bfloat16)
+        flying3.append(start(2, part, s3[part], r3[part]))
+    base = 0
+    for part in range(3):
+        for cp in flying3[part]:
+            cp.wait_recv()
+        total = s3[part][place[ORDERS[part][2]]].astype(f32)
+        for k in range(3):
+            total = total + r3[part][k].astype(f32)
+        out[base:base + PARTS[part]] = total
+        base += PARTS[part]
+    for cp in core_copies:
+        cp.wait_send()
+    for copies in flying + flying2 + flying3:
+        for cp in copies:
+            cp.wait_send()
+
+def reduce_scatter(grads):
+    bf16 = jnp.bfloat16
+    buf = lambda *lead: [pltpu.VMEM(lead + (rows, 128), bf16) for rows in PARTS]
+    return pl.pallas_call(
+        reduce_scatter_kernel,
+        out_shape=jax.ShapeDtypeStruct((ROWS, 128), jnp.float32),
+        in_specs=[pl.BlockSpec(memory_space=pltpu.VMEM)],
+        out_specs=pl.BlockSpec(memory_space=pltpu.VMEM),
+        scratch_shapes=[
+            pltpu.VMEM((4, 4, 4, ROWS, 128), bf16),
+            buf(4, 4, 4), buf(4, 4), buf(4), buf(3, 4, 4), buf(3, 4), buf(3),
+            pltpu.SemaphoreType.DMA((4,)), pltpu.SemaphoreType.DMA((4,)),
+            pltpu.SemaphoreType.DMA((27,)), pltpu.SemaphoreType.DMA((27,)),
+        ],
+        compiler_params=pltpu.CompilerParams(collective_id=1, has_side_effects=True, vmem_limit_bytes=32 * 2**20),
+        name="grad_reduce_scatter",
+    )(grads)
+
+
+def slide_kernel(count, embeds, own_pick, take_pick, pos_code, taps, weight, bias, cot, feature, embed_grad,
+                 emb_all, rows_mine, rows_all, wide, grad_wide, grad_mine, grad_all,
+                 send1, recv1, send2, recv2, send3, recv3):
+    f32, bf16 = jnp.float32, jnp.bfloat16
+    dp, group = lax.axis_index("dp"), lax.axis_index("group")
+    barrier = pltpu.get_barrier_semaphore()
+    dp_peers = [lax.rem(dp + k, 8) for k in range(1, 8)]
+    group_peers = [lax.rem(group + k, 16) for k in range(1, 16)]
+    for to in dp_peers:
+        pl.semaphore_signal(barrier, inc=1, device_id=(to, group), device_id_type=MESH)
+    for to in group_peers:
+        pl.semaphore_signal(barrier, inc=1, device_id=(dp, to), device_id_type=MESH)
+    pl.semaphore_wait(barrier, 22)
+
+    def over_dp(source, landing, send, recv):
+        copies = []
+        for k, to in enumerate(dp_peers):
+            cp = pltpu.make_async_remote_copy(src_ref=source, dst_ref=landing.at[dp], send_sem=send.at[k], recv_sem=recv.at[k], device_id=(to, group), device_id_type=MESH)
+            cp.start()
+            copies.append(cp)
+        landing[dp] = source[...]
+        for cp in copies:
+            cp.wait()
+
+    over_dp(embeds, emb_all, send1, recv1)
+    places = count[0]
+    own = jnp.dot(own_pick[...], emb_all[...].reshape(64, 768).astype(bf16), preferred_element_type=f32)
+    slot = lax.broadcasted_iota(jnp.int32, (8, 768), 0)
+    here = slot * 16 + group < places
+    rows_mine[...] = jnp.where(here, (own + pos_code[...]).astype(bf16).astype(f32), 0.0)
+    copies = []
+    for k, to in enumerate(group_peers):
+        cp = pltpu.make_async_remote_copy(src_ref=rows_mine, dst_ref=rows_all.at[group], send_sem=send2.at[k], recv_sem=recv2.at[k], device_id=(dp, to), device_id_type=MESH)
+        cp.start()
+        copies.append(cp)
+    rows_all[group] = rows_mine[...]
+    for cp in copies:
+        cp.wait()
+
+    def widen(block, target):
+        first, last = slot == 0, slot == 7
+        target[9:25] = block
+        for g in range(9):
+            target[g] = jnp.where(first, 0.0, pltpu.roll(block[g + 7], 1, 0))
+            target[25 + g] = jnp.where(last, 0.0, pltpu.roll(block[g], 7, 0))
+
+    rows = rows_all[...]
+    widen(rows, wide)
+    mixed = rows
+    for k in range(7):
+        mixed = mixed + taps[k] * wide[3 * k:3 * k + 16]
+    mixed = mixed.astype(bf16).reshape(128, 768)
+    pre = jnp.dot(mixed, weight[...], preferred_element_type=f32) + bias[...]
+    row = lax.broadcasted_iota(jnp.int32, (128, 768), 0)
+    place = lax.rem(row, 8) * 16 + lax.div(row, 8)
+    share = jnp.where(place < places, 1.0, 0.0) / places.astype(f32)
+    phi = 0.5 * (1.0 + lax.erf(pre * HALF_ROOT))
+    feature[...] = jnp.sum(pre * phi * share, axis=0, keepdims=True)
+    slope = phi + pre * INV_ROOT_TAU * jnp.exp(-0.5 * pre * pre)
+    grad_agg = (cot[...] * share * slope).astype(bf16)
+    grad_mixed = lax.dot_general(grad_agg, weight[...], (((1,), (1,)), ((), ())), preferred_element_type=f32)
+    widen(grad_mixed.reshape(16, 8, 768), grad_wide)
+    mine = grad_wide[9 + group]
+    total = mine
+    for k in range(7):
+        total = total + taps[k] * grad_wide[group + 18 - 3 * k]
+    grad_mine[...] = jnp.where(here, total.astype(bf16).astype(f32), 0.0)
+    over_dp(grad_mine, grad_all, send3, recv3)
+    embed_grad[...] = jnp.dot(take_pick[...], grad_all[...].reshape(64, 768).astype(bf16), preferred_element_type=f32)
+
+def slide_step(count, embeds, own_pick, take_pick, pos_code, taps, weight, bias, cot):
+    f32 = jnp.float32
+    vm = pl.BlockSpec(memory_space=pltpu.VMEM)
+    sem = lambda n: pltpu.SemaphoreType.DMA((n,))
+    return pl.pallas_call(
+        slide_kernel,
+        out_shape=(jax.ShapeDtypeStruct((1, 768), f32), jax.ShapeDtypeStruct((8, 768), f32)),
+        in_specs=[pl.BlockSpec(memory_space=pltpu.SMEM)] + [vm] * 8,
+        out_specs=(vm, vm),
+        scratch_shapes=[
+            pltpu.VMEM((8, 8, 768), f32), pltpu.VMEM((8, 768), f32), pltpu.VMEM((16, 8, 768), f32),
+            pltpu.VMEM((34, 8, 768), f32), pltpu.VMEM((34, 8, 768), f32),
+            pltpu.VMEM((8, 768), f32), pltpu.VMEM((8, 8, 768), f32),
+            sem(7), sem(7), sem(15), sem(15), sem(7), sem(7),
+        ],
+        compiler_params=pltpu.CompilerParams(collective_id=2, has_side_effects=True, vmem_limit_bytes=32 * 2**20),
+        name="slide_step",
+    )(count, embeds, own_pick, take_pick, pos_code, taps.reshape(7, 1, 768), weight, bias.reshape(1, 768), cot)
+
+
+def sender_table(my_list):
     dest_dev = jnp.where(my_list >= 0, my_list // PROC, -1)
-    is_hit = dest_dev[None, :] == jnp.arange(slides, dtype=jnp.int32)[:, None]
-    order_rank = jnp.cumsum(is_hit.astype(jnp.int32), axis=1) - 1
-    chosen = is_hit[:, None, :] & (
-        order_rank[:, None, :] == jnp.arange(places, dtype=jnp.int32)[None, :, None]
-    )
-    return chosen.reshape(slides * places, -1)
-
-
-def receiver_table(route_rows, my_slide, places):
-    dest_dev = jnp.where(route_rows >= 0, route_rows // PROC, -1)
-    is_hit = dest_dev == my_slide
-    order_rank = jnp.cumsum(is_hit.astype(jnp.int32), axis=1) - 1
-    chosen = is_hit[:, None, :] & (
-        order_rank[:, None, :] == jnp.arange(places, dtype=jnp.int32)[None, :, None]
-    )
-    target = jnp.sum(jnp.where(chosen, (route_rows % PROC)[:, None, :], 0), axis=2).reshape(-1)
-    is_used = jnp.any(chosen, axis=2).reshape(-1)
+    return dest_dev[None, :] == jnp.arange(8, dtype=jnp.int32)[:, None]
+
+
+def receiver_table(route_rows, my_slide):
+    local = route_rows - my_slide * PROC
+    hit = (local >= 0) & (local < PROC)
+    target = jnp.sum(jnp.where(hit, local, 0), axis=1)
+    is_used = jnp.any(hit, axis=1)
     return (target[None, :] == jnp.arange(PROC, dtype=jnp.int32)[:, None]) & is_used[None, :]
 
 
@@ -237,58 +398,36 @@
         layer_scale,
         head_weight,
     )
-    slides = lax.axis_size("dp")
-    members = lax.axis_size("group")
     my_slide = lax.axis_index("dp")
-    my_member = lax.axis_index("group")
     slot_count = tile_maps.shape[0]
-    embed_width = head_weight.shape[1]
-    places = slot_count // slides
     route_rows = routing[:, 0, :]
     my_list = lax.dynamic_index_in_dim(route_rows, my_slide, 0, keepdims=False)
-    send_pick = sender_table(my_list, slides, places).astype(jnp.bfloat16)
-    take_bool = receiver_table(route_rows, my_slide, places)
+    send_pick = sender_table(my_list).astype(jnp.bfloat16)
+    take_bool = receiver_table(route_rows, my_slide)
     take_pick = take_bool.astype(jnp.bfloat16)
     filled = jnp.any(take_bool, axis=1)
+    lanes = jnp.arange(64, dtype=jnp.int32)
+    place_code = jnp.where(lanes % 8 < PROC, lanes // 8 * PROC + lanes % 8, -2)
+    own_pick = (my_list[:, None] == place_code[None, :]).astype(jnp.bfloat16)
+    wanted = jnp.where(jnp.arange(8) < PROC, my_slide * PROC + jnp.arange(8), -2)
+    grad_pick = (wanted[:, None] == route_rows.reshape(64)[None, :]).astype(jnp.bfloat16)
+    pos_code = position_code(positions)
     packed = jnp.dot(
         send_pick, tile_maps.reshape(slot_count, -1), preferred_element_type=jnp.float32
     ).astype(jnp.bfloat16)
-    packed = packed.reshape((slides * places,) + tile_maps.shape[1:])
+    packed = packed.reshape(tile_maps.shape)
     arrived = lax.all_to_all(packed, "dp", split_axis=0, concat_axis=0, tiled=True)
     work_tiles = jnp.dot(
-        take_pick, arrived.reshape(slides * places, -1), preferred_element_type=jnp.float32
+        take_pick, arrived.reshape(slot_count, -1), preferred_element_type=jnp.float32
     ).astype(jnp.bfloat16)
-    work_tiles = work_tiles.reshape((take_pick.shape[0],) + tile_maps.shape[1:])
+    work_tiles = work_tiles.reshape((PROC,) + tile_maps.shape[1:])
     section_out, tile_embed, saved_acts = block_forward(work_tiles, *params)
     tile_out = jnp.where(filled[:, None, None, None], section_out, jnp.zeros((), jnp.bfloat16))
-    returned = contract_rows(take_pick, tile_embed).astype(jnp.bfloat16)
-    came_back = lax.all_to_all(returned, "dp", split_axis=0, concat_axis=0, tiled=True)
-    own_emb = contract_rows(send_pick, came_back)
-    slide_count = counts[0]
-    own_seq = jnp.arange(slot_count, dtype=jnp.int32) * members + my_member
-    own_present = own_seq < slide_count
-    slide_rows = jnp.where(
-        own_present[:, None],
-        (own_emb + position_code(positions)).astype(jnp.bfloat16),
-        jnp.zeros((), jnp.bfloat16),
-    )
-    gathered = lax.all_gather(
-        slide_rows.reshape(slot_count, 1, embed_width), "group", axis=1, tiled=True
-    )
-    sequence = gathered.reshape(slot_count * members, embed_width)
-    seq_present = jnp.arange(slot_count * members, dtype=jnp.int32) < slide_count
-    slide_cot = cotangent[0]
-    feature, seq_grad = slide_pass(
-        sequence, seq_present, slide_count, slide_cot, slide_taps, slide_weight, slide_bias
-    )
-    own_grad = lax.dynamic_index_in_dim(
-        seq_grad.reshape(slot_count, members, embed_width), my_member, 1, keepdims=False
-    )
-    outgoing = jnp.dot(send_pick, own_grad, preferred_element_type=jnp.float32).astype(jnp.bfloat16)
-    incoming = lax.all_to_all(outgoing, "dp", split_axis=0, concat_axis=0, tiled=True)
-    embed_grad = jnp.dot(take_pick, incoming, preferred_element_type=jnp.float32).astype(
-        jnp.bfloat16
-    )
+    embeds = jnp.pad(tile_embed.astype(jnp.float32), ((0, 4), (0, 0)))
+    feature, embed_grad = slide_step(
+        counts, embeds, own_pick, grad_pick, pos_code, slide_taps, slide_weight, slide_bias, cotangent
+    )
+    embed_grad = embed_grad[:PROC].astype(jnp.bfloat16)
     source_tiles, _ = lax.optimization_barrier((work_tiles, embed_grad))
     kept_acts = block_forward(source_tiles, *params)[2]
     expand_grad, reduce_grad, depth_grad = block_backward(
@@ -301,12 +440,19 @@
         layer_scale,
         head_weight,
     )
-    shares = (
-        lax.psum_scatter(expand_grad.reshape(-1), ("dp", "group"), scatter_dimension=0, tiled=True),
-        lax.psum_scatter(reduce_grad.reshape(-1), ("dp", "group"), scatter_dimension=0, tiled=True),
-        lax.psum_scatter(depth_grad.reshape(-1), ("dp", "group"), scatter_dimension=0, tiled=True),
-    )
-    return (tile_out, feature[None, :], shares[0], shares[1], shares[2])
+    depth_rows = jnp.pad(depth_grad.reshape(128, 147), ((0, 0), (0, 8 * 128 - 147)))
+    grads = jnp.concatenate(
+        [expand_grad.reshape(128, 36, 128), reduce_grad.reshape(128, 36, 128), depth_rows.reshape(128, 8, 128)],
+        axis=1,
+    ).astype(jnp.bfloat16)
+    shares = reduce_scatter(grads.reshape(4, 2, 4, 4, ROWS, 128))
+    return (
+        tile_out,
+        feature,
+        shares[0:36].reshape(-1),
+        shares[36:72].reshape(-1),
+        shares[72:80].reshape(-1)[:147],
+    )
 
 
 def solution(mesh):

time: 373 us -> 173 us (0.46)
  waiting for transfers between devices: 168 us -> 16.4 us
  Pallas kernels: 0 us -> 45.9 us
  local copies, waits for them, and re-layouts: 57.7 us -> 20.3 us
  blocking collectives: 32.8 us -> 0 us
  between operations: 15.8 us -> 3.58 us
  starting transfers between devices: 10.2 us -> 6.11 us
    unnamed x2 -> x0, waiting for transfers between devices: 151 us -> none
    pallas_call x0 -> x2, Pallas kernels: none -> 45.9 us  [the longest x1 23.4 us: slide_step(): pl.pallas_call(slide_kernel, out_shape=(jax.ShapeDtypeStruct((1, 768), f3...]
    another operation x50, local copies, waits for them, and re-layouts: 30.5 us -> 0.48 us  [block_backward(): return (expand_grad, reduce_grad, jnp.stack(tap_grads))]
    all_gather x1 -> x0, blocking collectives: 19.9 us -> none  [on_device(): lax.all_gather(slide_rows.reshape(slot_count, 1, embed_width), 'group', a...]
    all_to_all x1 -> x0, blocking collectives: 12.9 us -> none  [on_device(): lax.all_to_all(outgoing, 'dp', split_axis=0, concat_axis=0, tiled=True)]
    concatenate x0 -> x2, local copies, waits for them, and re-layouts: none -> 6.03 us  [on_device(): jnp.concatenate([expand_grad.reshape(128, 36, 128), reduce_grad.reshape(1...]
    all_to_all x1 -> x0, waiting for transfers between devices: 4.61 us -> none  [on_device(): lax.all_to_all(returned, 'dp', split_axis=0, concat_axis=0, tiled=True)]
    reshape x4 -> x6, local copies, waits for them, and re-layouts: 6.83 us -> 2.26 us  [the longest x1 1.35 us: on_device(): packed = packed.reshape(tile_maps.shape)]
  transfers between devices with their start and end apart: 3 -> 1, of which waited for: 3 -> 1; matrix products, arithmetic and copies ran while one was open for 2% -> 2% of each run, Pallas kernels for 0% -> 0%
where the time goes in v1:
time: 173 us
  other arithmetic  52.8 us (31%)
  Pallas kernels  45.9 us (27%)
  matrix products  27.5 us (16%)
  local copies, waits for them, and re-layouts  20.3 us (12%)
  waiting for transfers between devices  16.4 us (9%)
  starting transfers between devices  6.11 us (4%)
  between operations  3.58 us (2%)
    reduce_sum x2, other arithmetic, block_forward(): chan_mean = jnp.mean(depth_out, axis=1, keepdims=True)  26.7 us
    pallas_call x1, Pallas kernels, slide_step(): pl.pallas_call(slide_kernel, out_shape=(jax.ShapeDtypeStruct((1, 768), f3...  23.4 us
    pallas_call x1, Pallas kernels, reduce_scatter(): pl.pallas_call(reduce_scatter_kernel, out_shape=jax.ShapeDtypeStruct((ROW...  22.4 us
    all_to_all x1, waiting for transfers between devices, on_device(): lax.all_to_all(packed, 'dp', split_axis=0, concat_axis=0, tiled=True)  16.4 us
    reduce_sum x3, other arithmetic, block_backward(): jnp.sum(grad_depthwise * padded[:, tap_row:tap_row + tile_side, tap_col:t...  12.6 us
    dot_general x2, matrix products, block_forward(): jnp.dot(hidden, reduce_weight, preferred_element_type=jnp.float32)  7.27 us
    unnamed x243, local copies, waits for them, and re-layouts  6.59 us
    dot_general x3, matrix products, contract_cols(): lax.dot_general(left_side, right_side, (((1,), (1,)), ((), ())), preferre...  6.48 us
  transfers between devices with their start and end apart: 1, of which 1 were waited for; matrix products, arithmetic and copies ran while one was open for 2% of the time, Pallas kernels for 0%

profile of v1, /device:TPU:1, one launch (start us, length us, event | category | flops | bytes accessed | tf_op | source)
XLA Modules:
  0.0 172.6 jit_solution(11654578752286469499)
XLA Ops:
  0.7 2.4 %copy.29 = bf16[1,8,256,384]{3,1,2,0:T(8,128)(2,1)S(1)} copy(bf16[1,8,256,384]{3,2,1,0:T(8,128)(2,1)} %bitcast.155) | data formatting | bytes 3145728
  5.0 6.1 %all-to-all-start = ((bf16[8,16,16,384]{3,2,1,0:T(8,128)(2,1)}), bf16[8,16,16,384]{3,2,1,0:T(8,128)(2,1)}, u32[]{:S(2)}, u32[]{:S(2)}) async-start(bf16[8,16,16,384]{3,2,1,0:T(8,128)(2,1)} %copy.28), calls=%async_computation | async-start | bytes 3145728 | tf_op jit(solution)/shard_map/all_to_all | solution.py:419
  15.5 16.4 %all-to-all-done = bf16[8,16,16,384]{3,2,1,0:T(8,128)(2,1)} async-done(((bf16[8,16,16,384]{3,2,1,0:T(8,128)(2,1)}), bf16[8,16,16,384]{3,2,1,0:T(8,128)(2,1)}, u32[]{:S(2)}, u32[]{:S(2)}) %all-to-all-start) | async-done | bytes 1572896 | tf_op jit(solution)/shard_map/all_to_all | solution.py:419
  32.0 2.3 %copy.30 = bf16[1,8,256,384]{3,1,2,0:T(8,128)(2,1)S(1)} copy(bf16[1,8,256,384]{3,2,1,0:T(8,128)(2,1)} %bitcast.20) | data formatting | bytes 3145728
  37.0 13.6 %fusion.142 = (f32[4,16,16]{2,1,0:T(8,128)S(1)}, f32[4,16,16,384]{3,2,1,0:T(8,128)}) fusion(f32[384]{0:T(512)S(1)} %get-tuple-element.109, f32[384]{0:T(512)S(1)} %get-tuple-element.110, f32[384]{0:T(512)S(1)} %get-tuple-element.63, f32[384]{0:T(512)S(1)} %get-tuple-element.64, f32[384]{0:T(512)S(1)} %get-tuple-element.65, f32[384]{0:T(512)S(1)} %get-tuple-element.66, ...), kind=kLoop, calls=%fused_computation.453 | loop fusion | flops 58194944 | bytes 2440192 | tf_op jit(solution)/shard_map/reduce_sum | solution.py:78
  52.6 2.6 %fusion.112 = bf16[1024,384]{1,0:T(8,128)(2,1)} fusion(f32[4,16,16,384]{3,2,1,0:T(8,128)} %get-tuple-element.117, f32[384]{0:T(512)S(1)} %copy-done.86, f32[384]{0:T(512)S(1)} %copy-done.88, f32[1024]{0:T(1024)S(1)} %rsqrt.23, f32[1024]{0:T(1024)S(1)} %div.65), kind=kLoop, calls=%fused_computation.319 | loop fusion | flops 1966080 | bytes 2370560 | tf_op jit(solution)/shard_map/convert_element_type | solution.py:82
  55.2 5.5 %add_convert_fusion.1 = bf16[1024,384]{1,0:T(8,128)(2,1)S(1)} fusion(f32[1024,384]{1,0:T(8,128)} %reshape.326, bf16[1536,384]{1,0:T(8,128)(2,1)} %param.28, bf16[1024,384]{1,0:T(8,128)(2,1)} %fusion.112, bf16[384,1536]{1,0:T(8,128)(2,1)S(1)} %copy-done, f32[1536]{0:T(1024)S(1)} %copy-done.112, f32[384]{0:T(512)S(1)} %copy-done.114, f32[384]{0:T(512)S(1)} %copy-done.116), kind=kOutput, calls=%fused_computation.326 | convolution fusion | flops 2426929152 | bytes 5514240 | tf_op jit(solution)/shard_map/dot_general | solution.py:85
  61.1 2.8 %bitcast_reduce_fusion = f32[4,768]{1,0:T(4,128)S(1)} fusion(bf16[1024,384]{1,0:T(8,128)(2,1)S(1)} %add_convert_fusion.1, bf16[384,768]{1,0:T(8,128)(2,1)} %param.31), kind=kOutput, calls=%fused_computation.113 | convolution fusion | flops 607908864 | bytes 1388544 | tf_op jit(solution)/shard_map/dot_general | solution.py:89
  64.0 23.4 %slide_step.1 = (f32[1,768]{1,0:T(1,128)S(1)}, f32[8,768]{1,0:T(8,128)S(1)}) custom-call(s32[1]{0:T(128)S(6)} %copy.34.count, f32[8,768]{1,0:T(8,128)S(1)} %pad_convert_fusion.embeds, bf16[8,64]{1,0:T(8,128)(2,1)S(1)} %get-tuple-element.130.own_pick, bf16[8,64]{1,0:T(8,128)(2,1)S(1)} %get-tuple-element.129.take_pick, ...), custom_call_target="tpu_custom_call" | custom-call | tf_op jit(solution)/shard_map/slide_step/pallas_call | solution.py:340
  88.3 13.1 %fusion.140 = (f32[4,16,16]{2,1,0:T(8,128)S(1)}, f32[4,16,16,384]{3,2,1,0:T(8,128)S(1)}) fusion(f32[384]{0:T(512)S(1)} %copy-done.21, f32[384]{0:T(512)S(1)} %copy-done.23, f32[384]{0:T(512)S(1)} %copy-done.65, f32[384]{0:T(512)S(1)} %copy-done.67, f32[384]{0:T(512)S(1)} %copy-done.69, f32[384]{0:T(512)S(1)} %copy-done.71, f32[384]{0:T(512)S(1)} %copy-done.73, ...), kind=kLoop, calls=%fused_computation.452 | loop fusion | flops 58194944 | bytes 2440192 | tf_op jit(solution)/shard_map/reduce_sum | solution.py:78
  106.6 2.7 %multiply_convert_fusion = (bf16[1024,1536]{1,0:T(8,128)(2,1)S(1)}, f32[1024,1536]{1,0:T(8,128)S(1)}) fusion(f32[1536]{0:T(1024)S(1)} %copy-done.113, bf16[1024,384]{1,0:T(8,128)(2,1)S(1)} %add_convert_fusion, bf16[384,1536]{1,0:T(8,128)(2,1)S(1)} %copy-done), kind=kOutput, calls=%fused_computation.104 | convolution fusion | flops 1217396736 | bytes 11409408 | tf_op jit(solution)/shard_map/dot_general | solution.py:83
  109.4 1.8 %fusion.107 = bf16[1024,384]{1,0:T(8,128)(2,1)S(1)} fusion(bf16[1024,1536]{1,0:T(8,128)(2,1)S(1)} %get-tuple-element.126, bf16[1536,384]{1,0:T(8,128)(2,1)S(1)} %copy-done.110, bf16[4,16,16,384]{3,2,1,0:T(8,128)(2,1)S(1)} %bitcast.147, f32[384]{0:T(512)S(1)} %copy-done.115, f32[384]{0:T(512)S(1)} %copy-done.117), kind=kOutput, calls=%fused_computation.312 | convolution fusion | flops 1209925632 | bytes 5901312 | tf_op jit(solution)/shard_map/dot_general | solution.py:85
  111.3 1.8 %fusion.9 = bf16[1024,768]{1,0:T(8,128)(2,1)S(1)} fusion(bf16[1024,384]{1,0:T(8,128)(2,1)S(1)} %fusion.107, bf16[384,768]{1,0:T(8,128)(2,1)S(1)} %copy-done.111, f32[4,768]{1,0:T(4,128)S(1)} %copy-done.84), kind=kOutput, calls=%fused_computation.112 | convolution fusion | flops 611844096 | bytes 2961408 | tf_op jit(solution)/shard_map/dot_general | solution.py:89
  114.1 2.9 %convolution_convert_fusion.2 = bf16[1536,384]{1,0:T(8,128)(2,1)} fusion(bf16[1024,1536]{1,0:T(8,128)(2,1)S(1)} %get-tuple-element.126, bf16[1024,384]{1,0:T(8,128)(2,1)S(1)} %multiply_convert_fusion.2), kind=kOutput, calls=%fused_computation.115 | convolution fusion | flops 1208549376 | bytes 5111808 | tf_op jit(solution)/shard_map/dot_general | solution.py:33
  117.0 3.5 %fusion.4 = bf16[1024,1536]{1,0:T(8,128)(2,1)S(1)} fusion(f32[1024,1536]{1,0:T(8,128)S(1)} %get-tuple-element.127, bf16[1024,384]{1,0:T(8,128)(2,1)S(1)} %multiply_convert_fusion.2, bf16[1536,384]{1,0:T(8,128)(2,1)S(1)} %copy-done.110, f32[1536]{0:T(1024)S(1)} %copy-done.113), kind=kOutput, calls=%fused_computation.103 | convolution fusion | flops 1225261056 | bytes 11409408 | tf_op jit(solution)/shard_map/dot_general | solution.py:39
  120.4 2.4 %convolution_convert_fusion.3 = bf16[384,1536]{1,0:T(8,128)(2,1)} fusion(bf16[1024,384]{1,0:T(8,128)(2,1)S(1)} %add_convert_fusion, bf16[1024,1536]{1,0:T(8,128)(2,1)S(1)} %fusion.4), kind=kOutput, calls=%fused_computation.116 | convolution fusion | flops 1208549376 | bytes 5111808 | tf_op jit(solution)/shard_map/dot_general | solution.py:33
  122.9 2.0 %fusion.139 = (f32[1024]{0:T(1024)S(1)}, f32[1024]{0:T(1024)S(1)}, f32[1024,384]{1,0:T(8,128)S(1)}) fusion(f32[1024]{0:T(1024)S(1)} %rsqrt.25, f32[1024]{0:T(1024)S(1)} %div.73, f32[4,16,16,384]{3,2,1,0:T(8,128)S(1)} %get-tuple-element.115, f32[384]{0:T(512)S(1)} %copy-done.89, bf16[1024,1536]{1,0:T(8,128)(2,1)S(1)} %fusion.4, ...), kind=kOutput, calls=%fused_computation.451 | convolution fusion | flops 1210316800 | bytes 7489024 | tf_op jit(solution)/shard_map/dot_general | solution.py:39
  124.9 6.2 %fusion.105 = (bf16[384]{0:T(512)(128)(2,1)}, bf16[384]{0:T(512)(128)(2,1)}, bf16[384]{0:T(512)(128)(2,1)}, bf16[384]{0:T(512)(128)(2,1)}, bf16[384]{0:T(512)(12...) fusion(bf16[4,16,16,384]{3,2,1,0:T(8,128)(2,1)S(1)} %bitcast.14, ...), kind=kLoop, calls=%fused_computation.309 | loop fusion | flops 23586048 | bytes 5535232 | tf_op jit(solution)/shard_map/reduce_sum | solution.py:139
  131.1 2.6 %fusion.104 = (bf16[384]{0:T(512)(128)(2,1)S(1)}, bf16[384]{0:T(512)(128)(2,1)S(1)}, bf16[384]{0:T(512)(128)(2,1)S(1)}, bf16[384]{0:T(512)(128)(2,1)S(1)}, bf16[...) fusion(bf16[4,16,16,384]{3,2,1,0:T(8,128)(2,1)S(1)} %bitcast.14, ...), kind=kLoop, calls=%fused_computation.308 | loop fusion | flops 15330432 | bytes 2369280 | tf_op jit(solution)/shard_map/reduce_sum | solution.py:139
  133.7 3.7 %fusion.106 = (bf16[384]{0:T(512)(128)(2,1)S(1)}, bf16[384]{0:T(512)(128)(2,1)S(1)}, bf16[384]{0:T(512)(128)(2,1)S(1)}, bf16[384]{0:T(512)(128)(2,1)S(1)}, bf16[...) fusion(bf16[4,16,16,384]{3,2,1,0:T(8,128)(2,1)S(1)} %bitcast.15, ...), kind=kLoop, calls=%fused_computation.310 | loop fusion | flops 21226752 | bytes 2373120 | tf_op jit(solution)/shard_map/reduce_sum | solution.py:139
  137.7 2.4 %concatenate.16 = bf16[4,2,4,4,36,128]{5,4,3,2,1,0:T(8,128)(2,1)S(1)} reshape(bf16[1536,384]{1,0:T(8,128)(2,1)} %convolution_convert_fusion.2) | data formatting | bytes 2359296 | tf_op jit(solution)/shard_map/concatenate | solution.py:444
  141.3 3.6 %concatenate.15 = bf16[4,2,4,4,36,128]{5,4,3,2,1,0:T(8,128)(2,1)} reshape(bf16[384,1536]{1,0:T(8,128)(2,1)} %convolution_convert_fusion.3) | data formatting | bytes 2359296 | tf_op jit(solution)/shard_map/concatenate | solution.py:444
  145.1 2.3 %pad_maximum_fusion.grads = bf16[4,2,4,4,80,128]{5,4,3,2,1,0:T(8,128)(2,1)S(1)} fusion(bf16[4,2,4,4,8,128]{5,4,3,2,1,0:T(8,128)(2,1)S(1)} %bitcast.156, bf16[4,2,4,4,36,128]{5,4,3,2,1,0:T(8,128)(2,1)S(1)} %concatenate.16, bf16[4,2,4,4,36,128]{5,4,3,2,1,0:T(8,128)(2,1)} %concatenate.15), kind=kLoop, calls=%fused_computation.117 | loop fusion | flops 7864320 | bytes 5242880 | tf_op jit(solution)/shard_map/concatenate | solution.py:444
  147.3 22.4 %grad_reduce_scatter.1 = f32[80,128]{1,0:T(8,128)S(1)} custom-call(bf16[4,2,4,4,80,128]{5,4,3,2,1,0:T(8,128)(2,1)S(1)} %pad_maximum_fusion.grads), custom_call_target="tpu_custom_call" | custom-call | tf_op jit(solution)/shard_map/grad_reduce_scatter/pallas_call | solution.py:250
  (336 shorter events, 20.3 us)
Async XLA Ops:
  0.6 54.6 %copy-start = (bf16[384,1536]{1,0:T(8,128)(2,1)S(1)}, bf16[384,1536]{1,0:T(8,128)(2,1)}, u32[]{:S(2)}) copy-start(bf16[384,1536]{1,0:T(8,128)(2,1)} %param.26) | copy-start | bytes 3538948
  5.0 26.9 %all-to-all-start = ((bf16[8,16,16,384]{3,2,1,0:T(8,128)(2,1)}), bf16[8,16,16,384]{3,2,1,0:T(8,128)(2,1)}, u32[]{:S(2)}, u32[]{:S(2)}) async-start(bf16[8,16,16,384]{3,2,1,0:T(8,128)(2,1)} %copy.28), calls=%async_computation | async-start | bytes 3145728 | tf_op jit(solution)/shard_map/all_to_all | solution.py:419
  60.7 27.3 %copy-start.9 = (f32[384]{0:T(512)S(1)}, f32[384]{0:T(512)}, u32[]{:S(2)}) copy-start(f32[384]{0:T(512)} %copy-done.8) | copy-start | bytes 4612
  60.8 27.2 %copy-start.11 = (f32[384]{0:T(512)S(1)}, f32[384]{0:T(512)}, u32[]{:S(2)}) copy-start(f32[384]{0:T(512)} %copy-done.10) | copy-start | bytes 4612
  60.8 27.2 %copy-start.13 = (f32[384]{0:T(512)S(1)}, f32[384]{0:T(512)}, u32[]{:S(2)}) copy-start(f32[384]{0:T(512)} %copy-done.12) | copy-start | bytes 4612
  60.8 27.2 %copy-start.15 = (f32[384]{0:T(512)S(1)}, f32[384]{0:T(512)}, u32[]{:S(2)}) copy-start(f32[384]{0:T(512)} %copy-done.14) | copy-start | bytes 4612
  60.8 27.2 %copy-start.17 = (f32[384]{0:T(512)S(1)}, f32[384]{0:T(512)}, u32[]{:S(2)}) copy-start(f32[384]{0:T(512)} %copy-done.16) | copy-start | bytes 4612
  60.8 27.2 %copy-start.19 = (f32[384]{0:T(512)S(1)}, f32[384]{0:T(512)}, u32[]{:S(2)}) copy-start(f32[384]{0:T(512)} %copy-done.18) | copy-start | bytes 4612
  60.8 27.2 %copy-start.21 = (f32[384]{0:T(512)S(1)}, f32[384]{0:T(512)}, u32[]{:S(2)}) copy-start(f32[384]{0:T(512)} %copy-done.20) | copy-start | bytes 4612
  60.8 27.2 %copy-start.23 = (f32[384]{0:T(512)S(1)}, f32[384]{0:T(512)}, u32[]{:S(2)}) copy-start(f32[384]{0:T(512)} %copy-done.22) | copy-start | bytes 4612
  60.8 27.2 %copy-start.25 = (f32[384]{0:T(512)S(1)}, f32[384]{0:T(512)}, u32[]{:S(2)}) copy-start(f32[384]{0:T(512)} %copy-done.24) | copy-start | bytes 4612
  60.8 27.2 %copy-start.27 = (f32[384]{0:T(512)S(1)}, f32[384]{0:T(512)}, u32[]{:S(2)}) copy-start(f32[384]{0:T(512)} %copy-done.26) | copy-start | bytes 4612
  60.8 27.2 %copy-start.29 = (f32[384]{0:T(512)S(1)}, f32[384]{0:T(512)}, u32[]{:S(2)}) copy-start(f32[384]{0:T(512)} %copy-done.28) | copy-start | bytes 4612
  60.9 27.2 %copy-start.31 = (f32[384]{0:T(512)S(1)}, f32[384]{0:T(512)}, u32[]{:S(2)}) copy-start(f32[384]{0:T(512)} %copy-done.30) | copy-start | bytes 4612
  60.9 27.2 %copy-start.33 = (f32[384]{0:T(512)S(1)}, f32[384]{0:T(512)}, u32[]{:S(2)}) copy-start(f32[384]{0:T(512)} %copy-done.32) | copy-start | bytes 4612
  60.9 27.2 %copy-start.35 = (f32[384]{0:T(512)S(1)}, f32[384]{0:T(512)}, u32[]{:S(2)}) copy-start(f32[384]{0:T(512)} %copy-done.34) | copy-start | bytes 4612
  60.9 27.2 %copy-start.37 = (f32[384]{0:T(512)S(1)}, f32[384]{0:T(512)}, u32[]{:S(2)}) copy-start(f32[384]{0:T(512)} %copy-done.36) | copy-start | bytes 4612
  60.9 27.2 %copy-start.39 = (f32[384]{0:T(512)S(1)}, f32[384]{0:T(512)}, u32[]{:S(2)}) copy-start(f32[384]{0:T(512)} %copy-done.38) | copy-start | bytes 4612
  60.9 27.2 %copy-start.41 = (f32[384]{0:T(512)S(1)}, f32[384]{0:T(512)}, u32[]{:S(2)}) copy-start(f32[384]{0:T(512)} %copy-done.40) | copy-start | bytes 4612
  60.9 27.2 %copy-start.43 = (f32[384]{0:T(512)S(1)}, f32[384]{0:T(512)}, u32[]{:S(2)}) copy-start(f32[384]{0:T(512)} %copy-done.42) | copy-start | bytes 4612
  60.9 27.2 %copy-start.45 = (f32[384]{0:T(512)S(1)}, f32[384]{0:T(512)}, u32[]{:S(2)}) copy-start(f32[384]{0:T(512)} %copy-done.44) | copy-start | bytes 4612
  60.9 27.2 %copy-start.47 = (f32[384]{0:T(512)S(1)}, f32[384]{0:T(512)}, u32[]{:S(2)}) copy-start(f32[384]{0:T(512)} %copy-done.46) | copy-start | bytes 4612
  60.9 27.2 %copy-start.49 = (f32[384]{0:T(512)S(1)}, f32[384]{0:T(512)}, u32[]{:S(2)}) copy-start(f32[384]{0:T(512)} %copy-done.48) | copy-start | bytes 4612
  61.0 27.2 %copy-start.51 = (f32[384]{0:T(512)S(1)}, f32[384]{0:T(512)}, u32[]{:S(2)}) copy-start(f32[384]{0:T(512)} %copy-done.50) | copy-start | bytes 4612
  (95 other events, 1464.3 us)

commit v2 on v1

v2 whole, which is shorter than its diff:
```python
import math

import jax
import jax.numpy as jnp
from jax import lax
from jax.experimental import pallas as pl
from jax.experimental.pallas import tpu as pltpu
from jax.sharding import PartitionSpec as P

PROC = 4
EPSILON = 1e-06
HALF_ROOT = 0.7071067811865476
INV_ROOT_TAU = 0.3989422804014327
MESH = pl.DeviceIdType.MESH

WIDE = 14
STEP_U = 4
ROWS_STEP = STEP_U * 64
CHUNK = STEP_U * 16


def nt_dot(left, right):
    return lax.dot_general(left, right, (((1,), (1,)), ((), ())), preferred_element_type=jnp.float32)


def tn_dot(left, right):
    return lax.dot_general(left, right, (((0,), (0,)), ((), ())), preferred_element_type=jnp.float32)


def gelu_and_slope(pre):
    phi = 0.5 + 0.5 * lax.erf(pre * HALF_ROOT)
    return pre * phi, phi + pre * (INV_ROOT_TAU * jnp.exp(-0.5 * (pre * pre)))


def forward_kernel(routing, *refs):
    held, refs = refs[:11], refs[11:]
    forward_body(routing, held, *refs)


def forward_body(routing, held, tile_out, embed, cells, unit, inv_std, normed, hidden, slope, head_slope,
                   depth, section, embed_sum, arrived0, arrived1, arrived2, arrived3, leaving, send, recv, fetch, *local):
    f32, bf16 = jnp.float32, jnp.bfloat16
    dp, group = lax.axis_index("dp"), lax.axis_index("group")
    peers = [lax.rem(dp + k, 8) for k in range(8)]
    fetches = [pltpu.make_async_copy(a, b, fetch.at[i]) for i, (a, b) in enumerate(zip(held, local))]
    for copy in fetches:
        copy.start()
    tiles, depth_kernel, depth_bias, gain, shift, expand, expand_bias, reduce, reduce_bias, scale, head = local
    barrier = pltpu.get_barrier_semaphore()
    for to in peers[1:]:
        pl.semaphore_signal(barrier, inc=1, device_id=(to, group), device_id_type=MESH)

    def slot_for(to):
        found = 0
        for s in range(1, 8):
            local = routing[dp, 0, s] - to * PROC
            found = jnp.where((local >= 0) & (local < PROC), s, found)
        return found

    slots = [slot_for(to) for to in peers]
    source = []
    for q in range(PROC):
        found = -1
        for d in range(8):
            for s in range(8):
                found = jnp.where(routing[d, 0, s] == dp * PROC + q, d, found)
        source.append(found)

    arrived = (arrived0, arrived1, arrived2, arrived3)

    def chunk_copy(c, k):
        return pltpu.make_async_remote_copy(
            src_ref=leaving.at[k - 1, pl.ds(c * CHUNK, CHUNK)], dst_ref=arrived[c].at[dp], send_sem=send.at[c * 7 + k - 1],
            recv_sem=recv.at[c * 7 + k - 1], device_id=(peers[k], group), device_id_type=MESH)

    pl.semaphore_wait(barrier, 7)
    fetches[0].wait()

    for c in range(4):
        rows = pl.ds(c * CHUNK, CHUNK)
        for k in (4, 5, 3, 2, 6, 1, 7):
            leaving[k - 1, rows, :] = tiles[slots[k], rows, :]
            chunk_copy(c, k).start()
        arrived[c][dp] = tiles[slots[0], rows, :]
    edge = 3 * WIDE * 8
    cells[:, 0:edge] = jnp.zeros((3, edge, 128), f32)
    cells[:, edge + 16 * WIDE * 8:] = jnp.zeros((3, edge, 128), f32)
    zeros3 = jnp.zeros((3, 128), f32)

    def fill(c, i):
        u = c * STEP_U + i
        base = (u + 3) * (WIDE * 8)
        for q in range(PROC):
            src = source[q]
            row = arrived[c][jnp.maximum(src, 0), i * 16:i * 16 + 16, :].astype(f32)
            row = jnp.where(src >= 0, row, 0.0)
            for block in range(3):
                lanes = slice(block * 128, block * 128 + 128)
                cells[block, pl.ds(base + q * 2, 3, stride=8), :] = zeros3
                cells[block, pl.ds(base + 24 + q * 2, 11, stride=8), :] = row[0:11, lanes]
                cells[block, pl.ds(base + q * 2 + 1, 11, stride=8), :] = row[5:16, lanes]
                cells[block, pl.ds(base + 88 + q * 2 + 1, 3, stride=8), :] = zeros3

    def land(c):
        for k in range(1, 8):
            chunk_copy(c, k).wait_recv()
        for i in range(STEP_U):
            fill(c, i)

    for copy in fetches[1:]:
        copy.wait()
    land(0)
    embed_sum[...] = jnp.zeros((6, 8, 128), f32)

    def step(n, carry):
        start = pl.multiple_of(n * ROWS_STEP, ROWS_STEP)

        for c in range(1, 4):
            @pl.when(n == c - 1)
            def _():
                land(c)

        for block in range(3):
            lanes = pl.ds(block * 128, 128)
            for part in range(STEP_U // 2):
                acc = [jnp.zeros((8, 8, 128), f32) + depth_bias[lanes].reshape(1, 1, 128) for _ in range(2)]
                for a in range(8):
                    first = pl.multiple_of((n * STEP_U + part * 2 + a) * (WIDE * 8), 8)
                    x = cells[block, pl.ds(first, WIDE * 8), :].reshape(WIDE, 8, 128)
                    for i in range(2):
                        if 0 <= a - i < 7:
                            for b in range(7):
                                acc[i] = acc[i] + depth_kernel[pl.ds((a - i) * 7 + b, 1), lanes].reshape(1, 1, 128) * x[b:b + 8]
                for i in range(2):
                    depth[pl.ds((part * 2 + i) * 64, 64), lanes] = acc[i].reshape(64, 128)
        value = depth[...]
        centred = value - jnp.mean(value, axis=1, keepdims=True)
        inv = lax.rsqrt(jnp.mean(centred * centred, axis=1, keepdims=True) + EPSILON)
        z = centred * inv
        unit[pl.ds(start, ROWS_STEP), :] = z
        inv_std[pl.ds(start, ROWS_STEP), :] = jnp.broadcast_to(inv, (ROWS_STEP, 128))
        norm = (z * gain[...].reshape(1, 384) + shift[...].reshape(1, 384)).astype(bf16)
        normed[pl.ds(start, ROWS_STEP), :] = norm
        for m in range(6):
            cols = pl.ds(m * 256, 256)
            pre = jnp.dot(norm, expand[:, cols], preferred_element_type=f32) + expand_bias[cols].reshape(1, 256)
            act, grad = gelu_and_slope(pre)
            hidden[pl.ds(start, ROWS_STEP), cols] = act.astype(bf16)
            slope[pl.ds(start, ROWS_STEP), cols] = grad.astype(bf16)
        mlp = jnp.dot(hidden[pl.ds(start, ROWS_STEP), :], reduce[...], preferred_element_type=f32) + reduce_bias[...].reshape(1, 384)
        mlp = mlp * scale[...].reshape(1, 384)
        for i in range(STEP_U):
            first = pl.multiple_of((n * STEP_U + i + 3) * (WIDE * 8) + 24, 8)
            for block in range(3):
                section[block, pl.ds(i * 64, 64), :] = cells[block, pl.ds(first, 64), :] + mlp[i * 64:(i + 1) * 64, block * 128:block * 128 + 128]
        sec = jnp.concatenate([section[block] for block in range(3)], axis=1).astype(bf16)
        for m in range(3):
            cols = pl.ds(m * 256, 256)
            act, grad = gelu_and_slope(jnp.dot(sec, head[:, cols], preferred_element_type=f32))
            head_slope[pl.ds(start, ROWS_STEP), cols] = grad.astype(bf16)
            act = jnp.sum(act.reshape(STEP_U * 8, 8, 256), axis=0)
            for half in range(2):
                embed_sum[m * 2 + half] = embed_sum[m * 2 + half] + act[:, half * 128:half * 128 + 128]
        for i in range(STEP_U):
            for q in range(PROC):
                for block in range(3):
                    left = section[block, pl.ds(i * 64 + q * 2, 8, stride=8), :]
                    right = section[block, pl.ds(i * 64 + q * 2 + 1, 8, stride=8), :]
                    row = jnp.where(source[q] >= 0, jnp.concatenate([left, right], axis=0), 0.0)
                    tile_out[q, pl.ds(pl.multiple_of((n * STEP_U + i) * 16, 16), 16), pl.ds(block * 128, 128)] = row.astype(bf16)
        return carry

    lax.fori_loop(0, 16 // STEP_U, step, 0)
    means = [
        (embed_sum[block, pl.ds(0, 4, stride=2), :] + embed_sum[block, pl.ds(1, 4, stride=2), :]) * (1.0 / 256.0)
        for block in range(6)
    ]
    embed[...] = jnp.concatenate(means + [jnp.zeros((8, 128), f32)], axis=0).astype(bf16)

    for c in range(4):
        for k in range(1, 8):
            chunk_copy(c, k).wait_send()


def forward(routing, *arrays):
    f32, bf16 = jnp.float32, jnp.bfloat16
    vm = pl.BlockSpec(memory_space=pltpu.VMEM)
    out = lambda shape, kind: jax.ShapeDtypeStruct(shape, kind)
    return pl.pallas_call(
        forward_kernel,
        out_shape=(out((PROC, 256, 384), bf16), out((32, 128), bf16), out((3, 22 * WIDE * 8, 128), f32),
                   out((1024, 384), f32), out((1024, 128), f32), out((1024, 384), bf16),
                   out((1024, 1536), bf16), out((1024, 1536), bf16), out((1024, 768), bf16)),
        in_specs=[pl.BlockSpec(memory_space=pltpu.SMEM)] + [pl.BlockSpec(memory_space=pl.ANY)] * 11,
        out_specs=(vm,) * 9,
        scratch_shapes=[pltpu.VMEM((ROWS_STEP, 384), f32), pltpu.VMEM((3, ROWS_STEP, 128), f32), pltpu.VMEM((6, 8, 128), f32),
                        *[pltpu.VMEM((8, CHUNK, 384), bf16) for _ in range(4)], pltpu.VMEM((7, 256, 384), bf16),
                        pltpu.SemaphoreType.DMA((28,)), pltpu.SemaphoreType.DMA((28,)), pltpu.SemaphoreType.DMA((11,))]
        + [pltpu.VMEM(a.shape, a.dtype) for a in arrays],
        compiler_params=pltpu.CompilerParams(collective_id=3, has_side_effects=True, vmem_limit_bytes=60 * 2**20),
        name="block_forward",
    )(routing, *arrays)


def backward_kernel(embed_grad, cells, unit, inv_std, normed, hidden, slope, head_slope, gain, expand, reduce, scale,
                    head, shares, grad_mlp, grad_pre, depthwise, flat, flat2, taps):
    f32, bf16 = jnp.float32, jnp.bfloat16
    eg_row = jnp.concatenate([embed_grad[8 * block:8 * block + 8] for block in range(6)], axis=1) * (1.0 / 256.0)

    def first(n, carry):
        rows = pl.ds(pl.multiple_of(n * 256, 256), 256)
        gh = (eg_row[None] * head_slope[rows, :].astype(f32).reshape(32, 8, 768)).reshape(256, 768).astype(bf16)
        grad_mlp[rows, :] = (scale[...].reshape(1, 384) * nt_dot(gh, head[...])).astype(bf16)
        return carry

    lax.fori_loop(0, 4, first, 0)

    for m in range(6):
        cols = pl.ds(m * 256, 256)
        for n in range(4):
            rows = pl.ds(n * 256, 256)
            gp = nt_dot(grad_mlp[rows, :], reduce[cols, :]) * slope[rows, cols].astype(f32)
            grad_pre[rows, cols] = gp.astype(bf16)
        eg_m = tn_dot(normed[...], grad_pre[:, cols])
        for l in range(2):
            flat[pl.ds(m * 2 + l, 384, stride=12), :] = eg_m[:, l * 128:(l + 1) * 128]
    for m in range(6):
        rg_m = tn_dot(hidden[:, pl.ds(m * 256, 256)], grad_mlp[...])
        for l in range(3):
            flat2[pl.ds(m * 768 + l, 256, stride=3), :] = rg_m[:, l * 128:(l + 1) * 128]

    def second(n, carry):
        rows = pl.ds(pl.multiple_of(n * 256, 256), 256)
        w = nt_dot(grad_pre[rows, :], expand[...]) * gain[...].reshape(1, 384)
        z = unit[rows, :]
        inv = jnp.concatenate([inv_std[rows, :]] * 3, axis=1)
        depthwise[rows, :] = inv * (w - jnp.mean(w, axis=1, keepdims=True) - z * jnp.mean(w * z, axis=1, keepdims=True))
        return carry

    lax.fori_loop(0, 4, second, 0)

    for block in range(3):
        lanes = pl.ds(block * 128, 128)
        for a in range(7):
            def row(u, acc):
                g = depthwise[pl.ds(pl.multiple_of(u * 64, 64), 64), lanes].reshape(8, 8, 128)
                x = cells[block, pl.ds(pl.multiple_of((u + a) * (WIDE * 8), 8), WIDE * 8), :].reshape(WIDE, 8, 128)
                return tuple(acc[b] + jnp.sum(g * x[b:b + 8], axis=0) for b in range(7))
            acc = lax.fori_loop(0, 16, row, tuple(jnp.zeros((8, 128), f32) for _ in range(7)))
            for b in range(7):
                taps[pl.ds((a * 7 + b) * 3 + block, 1), :] = jnp.sum(acc[b], axis=0, keepdims=True)

    lane = lax.broadcasted_iota(jnp.int32, (8, 128), 1)
    flat2[4608:] = jnp.zeros((8, 128), f32)
    taps[147:] = jnp.zeros((13, 128), f32)
    for i in range(128):
        turn = (147 * i) % 128
        near = taps[pl.ds(147 * i // 128, 8), :]
        near = pltpu.roll(near, (128 - turn) % 128, 1) if turn else near
        near = jnp.where(lane < 128 - turn, near, pltpu.roll(near, 7, 0))
        shares[i, 0:32] = flat[pl.ds(i * 36, 32), :].astype(bf16)
        shares[i, 32:48] = jnp.concatenate([flat[pl.ds(i * 36 + 32, 4), :], near[0:4], flat2[pl.ds(i * 36, 8), :]], axis=0).astype(bf16)
        shares[i, 48:80] = flat2[pl.ds(i * 36 + 8, 32), :].astype(bf16)


def backward(embed_grad, acts, gain, expand, reduce, scale, head):
    f32, bf16 = jnp.float32, jnp.bfloat16
    vm = pl.BlockSpec(memory_space=pltpu.VMEM)
    row = lambda v: v
    return pl.pallas_call(
        backward_kernel,
        out_shape=jax.ShapeDtypeStruct((128, 80, 128), bf16),
        in_specs=[vm] * 13,
        out_specs=vm,
        scratch_shapes=[pltpu.VMEM((1024, 384), bf16), pltpu.VMEM((1024, 1536), bf16),
                        pltpu.VMEM((1024, 384), f32), pltpu.VMEM((4608, 128), f32), pltpu.VMEM((4616, 128), f32),
                        pltpu.VMEM((160, 128), f32)],
        compiler_params=pltpu.CompilerParams(vmem_limit_bytes=40 * 2**20),
        name="block_backward",
    )(embed_grad, *acts, row(gain), expand, reduce, row(scale), head)


def slide_kernel(count, routing, positions, embeds, taps, weight, bias, cot, feature, embed_grad,
                 emb_all, rows_mine, rows_all, wide, grad_wide, grad_mine, grad_all,
                 send1, recv1, send2, recv2, send3, recv3):
    f32, bf16, i32 = jnp.float32, jnp.bfloat16, jnp.int32
    dp, group = lax.axis_index("dp"), lax.axis_index("group")
    barrier = pltpu.get_barrier_semaphore()
    dp_peers = [lax.rem(dp + k, 8) for k in range(1, 8)]
    group_peers = [lax.rem(group + k, 16) for k in range(1, 16)]
    for to in dp_peers:
        pl.semaphore_signal(barrier, inc=1, device_id=(to, group), device_id_type=MESH)
    for to in group_peers:
        pl.semaphore_signal(barrier, inc=1, device_id=(dp, to), device_id_type=MESH)
    pl.semaphore_wait(barrier, 22)

    def over_dp(source, landing, send, recv):
        copies = []
        for k, to in enumerate(dp_peers):
            cp = pltpu.make_async_remote_copy(src_ref=source, dst_ref=landing.at[dp], send_sem=send.at[k], recv_sem=recv.at[k], device_id=(to, group), device_id_type=MESH)
            cp.start()
            copies.append(cp)
        landing[dp] = source[...]
        return copies

    def iota(shape, axis):
        return lax.broadcasted_iota(i32, shape, axis)

    copies1 = over_dp(embeds, emb_all, send1, recv1)
    places = count[0]

    row = iota((48, 128), 0)
    slot, block = row & 7, row >> 3
    channel = jnp.where(block >= 3, block - 3, block) * 128 + iota((48, 128), 1)
    spot = jnp.zeros((48, 128), i32)
    for s in range(8):
        spot = jnp.where(slot == s, jnp.where(block >= 3, positions[1, s], positions[0, s]), spot)
    frequency = jnp.exp((channel - (channel & 1)).astype(f32) * (-math.log(10000.0) / 384))
    angle = spot.astype(f32) * frequency
    pos_code = jnp.where((channel & 1) == 0, jnp.sin(angle), jnp.cos(angle))
    here = slot * 16 + group < places

    pick_row, pick_col = iota((48, 32), 0), iota((48, 32), 1)
    goes_to = jnp.full((48, 32), -1, i32)
    for s in range(8):
        goes_to = jnp.where((pick_row & 7) == s, routing[dp, 0, s], goes_to)
    goes_to = jnp.where((pick_row >> 3) == (pick_col >> 2), goes_to, -1)
    grad_row, grad_col = iota((48, 48), 0), iota((48, 48), 1)
    grad_place = jnp.where((grad_row >> 3) == (grad_col >> 3), dp * PROC + ((grad_row & 7) >> 1), -2)
    grad_picks = []
    for d in range(8):
        routed = jnp.full((48, 48), -1, i32)
        for s in range(8):
            routed = jnp.where((grad_col & 7) == s, routing[d, 0, s], routed)
        grad_picks.append(jnp.where(routed == grad_place, 1.0, 0.0).astype(bf16))

    for cp in copies1:
        cp.wait_recv()
    own = pos_code
    for e in range(8):
        pick = jnp.where(goes_to == e * PROC + (pick_col & 3), 1.0, 0.0).astype(bf16)
        own = own + jnp.dot(pick, emb_all[e], preferred_element_type=f32)
    rows_mine[...] = jnp.where(here, own, 0.0).astype(bf16)
    copies2 = []
    for k, to in enumerate(group_peers):
        cp = pltpu.make_async_remote_copy(src_ref=rows_mine, dst_ref=rows_all.at[group], send_sem=send2.at[k], recv_sem=recv2.at[k], device_id=(dp, to), device_id_type=MESH)
        cp.start()
        copies2.append(cp)
    rows_all[group] = rows_mine[...]
    for cp in copies2:
        cp.wait_recv()

    first, last = slot[0:8] == 0, slot[0:8] == 7

    def widen(block_rows, target):
        target[9:25] = block_rows
        for g in range(9):
            target[g] = jnp.where(first, 0.0, pltpu.roll(block_rows[g + 7], 1, 0))
            target[25 + g] = jnp.where(last, 0.0, pltpu.roll(block_rows[g], 7, 0))

    mixed = []
    for b in range(6):
        rows = rows_all[:, b * 8:b * 8 + 8, :].astype(f32)
        widen(rows, wide)
        total = rows
        for k in range(7):
            total = total + taps[pl.ds(k, 1), pl.ds(b * 128, 128)].reshape(1, 1, 128) * wide[3 * k:3 * k + 16]
        mixed.append(total.reshape(128, 128).astype(bf16))
    mixed = jnp.concatenate(mixed, axis=1)
    pre = jnp.dot(mixed, weight[...], preferred_element_type=f32) + bias[...].reshape(1, 768)
    seq_row = iota((128, 768), 0)
    share = jnp.where((seq_row & 7) * 16 + (seq_row >> 3) < places, 1.0, 0.0) / places.astype(f32)
    phi = 0.5 * (1.0 + lax.erf(pre * HALF_ROOT))
    slope = phi + pre * INV_ROOT_TAU * jnp.exp(-0.5 * pre * pre)
    grad_agg = (cot[...] * share * slope).astype(bf16)
    grad_mixed = lax.dot_general(grad_agg, weight[...], (((1,), (1,)), ((), ())), preferred_element_type=f32)
    grad_rows = []
    for b in range(6):
        widen(grad_mixed[:, b * 128:b * 128 + 128].reshape(16, 8, 128), grad_wide)
        total = grad_wide[9 + group]
        for k in range(7):
            total = total + taps[pl.ds(k, 1), pl.ds(b * 128, 128)] * grad_wide[group + 18 - 3 * k]
        grad_rows.append(total)
    grad_mine[...] = jnp.where(here, jnp.concatenate(grad_rows, axis=0), 0.0).astype(bf16)
    copies3 = over_dp(grad_mine, grad_all, send3, recv3)
    feature[...] = jnp.sum(pre * phi * share, axis=0, keepdims=True)
    for cp in copies3:
        cp.wait_recv()
    total = jnp.zeros((48, 128), f32)
    for d in range(8):
        total = total + jnp.dot(grad_picks[d], grad_all[d], preferred_element_type=f32)
    embed_grad[...] = total
    for cp in copies1 + copies2 + copies3:
        cp.wait_send()


def slide_step(count, routing, positions, embeds, taps, weight, bias, cot):
    f32, bf16 = jnp.float32, jnp.bfloat16
    vm = pl.BlockSpec(memory_space=pltpu.VMEM)
    sm = pl.BlockSpec(memory_space=pltpu.SMEM)
    sem = lambda n: pltpu.SemaphoreType.DMA((n,))
    return pl.pallas_call(
        slide_kernel,
        out_shape=(jax.ShapeDtypeStruct((1, 768), f32), jax.ShapeDtypeStruct((48, 128), f32)),
        in_specs=[sm] * 3 + [vm] * 5,
        out_specs=(vm, vm),
        scratch_shapes=[
            pltpu.VMEM((8, 32, 128), bf16), pltpu.VMEM((48, 128), bf16), pltpu.VMEM((16, 48, 128), bf16),
            pltpu.VMEM((34, 8, 128), f32), pltpu.VMEM((34, 8, 128), f32),
            pltpu.VMEM((48, 128), bf16), pltpu.VMEM((8, 48, 128), bf16),
            sem(7), sem(7), sem(15), sem(15), sem(7), sem(7),
        ],
        compiler_params=pltpu.CompilerParams(collective_id=2, has_side_effects=True, vmem_limit_bytes=16 * 2**20),
        name="slide_step",
    )(count, routing, positions, embeds, taps, weight, bias, cot)


PARTS = (32, 32, 16)
ORDERS = ("yxz", "xzy", "zyx")
ROWS = sum(PARTS)

def torus_place():
    dp, group = lax.axis_index("dp"), lax.axis_index("group")
    return {"y": lax.div(dp, 2), "c": lax.rem(dp, 2), "x": lax.div(group, 4), "z": lax.rem(group, 4)}

def torus_device(place, **moved):
    at = {**place, **moved}
    return (at["y"] * 2 + at["c"], at["x"] * 4 + at["z"])

def reduce_scatter_kernel(grads, out, core_in, s1, s2, s3, r1, r2, r3, core_send, core_recv, send, recv):
    place = torus_place()
    partner = torus_device(place, c=1 - place["c"])
    barrier = pltpu.get_barrier_semaphore()
    pl.semaphore_signal(barrier, inc=1, device_id=partner, device_id_type=MESH)
    for axis in "yxz":
        for k in (1, 2, 3):
            pl.semaphore_signal(barrier, inc=1, device_id=torus_device(place, **{axis: lax.rem(place[axis] + k, 4)}), device_id_type=MESH)
    pl.semaphore_wait(barrier, 10)

    core_copies = []
    for y in range(4):
        cp = pltpu.make_async_remote_copy(src_ref=grads.at[y, 1 - place["c"]], dst_ref=core_in.at[y], send_sem=core_send.at[y], recv_sem=core_recv.at[y], device_id=partner, device_id_type=MESH)
        cp.start()
        core_copies.append(cp)

    def start(stage, part, source, landing):
        axis = ORDERS[part][stage]
        made = []
        for k in (2, 1, 3):
            to = lax.rem(place[axis] + k, 4)
            cp = pltpu.make_async_remote_copy(src_ref=source.at[to], dst_ref=landing.at[k - 1], send_sem=send.at[stage * 9 + part * 3 + k - 1], recv_sem=recv.at[stage * 9 + part * 3 + k - 1], device_id=torus_device(place, **{axis: to}), device_id_type=MESH)
            cp.start()
            made.append(cp)
        return made

    f32 = jnp.float32
    for y in range(4):
        core_copies[y].wait_recv()
        for x in range(4):
            both = grads[y, place["c"], x].astype(f32) + core_in[y, x].astype(f32)
            both = both.astype(jnp.bfloat16)
            s1[0][y, x] = both[:, 0:32]
            s1[1][x, :, y] = both[:, 32:64]
            for z in range(4):
                s1[2][z, y, x] = both[z, 64:80]
    flying = [start(0, part, s1[part], r1[part]) for part in range(3)]
    flying2 = []
    for part in range(3):
        for cp in flying[part]:
            cp.wait_recv()
        mine = place[ORDERS[part][0]]
        for a in range(4):
            total = s1[part][mine, a].astype(f32)
            for k in range(3):
                total = total + r1[part][k, a].astype(f32)
            s2[part][a] = total.astype(jnp.bfloat16)
        flying2.append(start(1, part, s2[part], r2[part]))
    flying3 = []
    for part in range(3):
        for cp in flying2[part]:
            cp.wait_recv()
        mine = place[ORDERS[part][1]]
        total = s2[part][mine].astype(f32)
        for k in range(3):
            total = total + r2[part][k].astype(f32)
        s3[part][...] = total.astype(jnp.bfloat16)
        flying3.append(start(2, part, s3[part], r3[part]))
    base = 0
    for part in range(3):
        for cp in flying3[part]:
            cp.wait_recv()
        total = s3[part][place[ORDERS[part][2]]].astype(f32)
        for k in range(3):
            total = total + r3[part][k].astype(f32)
        out[base:base + PARTS[part]] = total
        base += PARTS[part]
    for cp in core_copies:
        cp.wait_send()
    for copies in flying + flying2 + flying3:
        for cp in copies:
            cp.wait_send()

def reduce_scatter(grads):
    bf16 = jnp.bfloat16
    buf = lambda *lead: [pltpu.VMEM(lead + (rows, 128), bf16) for rows in PARTS]
    return pl.pallas_call(
        reduce_scatter_kernel,
        out_shape=jax.ShapeDtypeStruct((ROWS, 128), jnp.float32),
        in_specs=[pl.BlockSpec(memory_space=pltpu.VMEM)],
        out_specs=pl.BlockSpec(memory_space=pltpu.VMEM),
        scratch_shapes=[
            pltpu.VMEM((4, 4, 4, ROWS, 128), bf16),
            buf(4, 4, 4), buf(4, 4), buf(4), buf(3, 4, 4), buf(3, 4), buf(3),
            pltpu.SemaphoreType.DMA((4,)), pltpu.SemaphoreType.DMA((4,)),
            pltpu.SemaphoreType.DMA((27,)), pltpu.SemaphoreType.DMA((27,)),
        ],
        compiler_params=pltpu.CompilerParams(collective_id=1, has_side_effects=True, vmem_limit_bytes=32 * 2**20),
        name="grad_reduce_scatter",
    )(grads)


def on_device(
    tile_maps,
    positions,
    counts,
    routing,
    depth_kernel,
    depth_bias,
    norm_gain,
    norm_shift,
    expand_weight,
    expand_bias,
    reduce_weight,
    reduce_bias,
    layer_scale,
    head_weight,
    slide_taps,
    slide_weight,
    slide_bias,
    cotangent,
):
    tile_out, embeds, *acts = forward(
        routing,
        tile_maps.reshape(8, 256, 384),
        depth_kernel,
        depth_bias,
        norm_gain,
        norm_shift,
        expand_weight,
        expand_bias,
        reduce_weight,
        reduce_bias,
        layer_scale,
        head_weight,
    )
    feature, embed_grad = slide_step(
        counts, routing, positions, embeds, slide_taps, slide_weight, slide_bias, cotangent
    )
    grads = backward(embed_grad, acts, norm_gain, expand_weight, reduce_weight, layer_scale, head_weight)
    shares = reduce_scatter(grads.reshape(4, 2, 4, 4, ROWS, 128))
    return (
        tile_out.reshape((PROC,) + tile_maps.shape[1:]),
        feature,
        shares[0:36].reshape(-1),
        shares[40:76].reshape(-1),
        shares[36:38].reshape(-1)[:147],
    )


def solution(mesh):
    return jax.shard_map(
        on_device,
        mesh=mesh,
        in_specs=(
            P(("dp", "group"), None, None, None),
            P(None, ("dp", "group")),
            P("dp"),
            P(None, "group", None),
            P(),
            P(),
            P(),
            P(),
            P(),
            P(),
            P(),
            P(),
            P(),
            P(),
            P(),
            P(),
            P(),
            P("dp", None),
        ),
        out_specs=(
            P(("dp", "group"), None, None, None),
            P("dp", None),
            P(("dp", "group")),
            P(("dp", "group")),
            P(("dp", "group")),
        ),
        check_vma=False,
    )
```

time: 173 us -> 114 us (0.66)
  Pallas kernels: 45.9 us -> 102 us
  other arithmetic: 52.8 us -> 0 us
  matrix products: 27.5 us -> 0 us
  waiting for transfers between devices: 16.4 us -> 0 us
  local copies, waits for them, and re-layouts: 20.3 us -> 10.3 us
  starting transfers between devices: 6.11 us -> 0 us
  between operations: 3.58 us -> 1.62 us
    pallas_call x0 -> x2, Pallas kernels: none -> 58.6 us  [the longest x1 37.9 us: forward(): pl.pallas_call(forward_kernel, out_shape=(out((PROC, 256, 384), bf16), ou...]
    reduce_sum x8 -> x0, other arithmetic: 42.3 us -> none  [the longest x2 26.7 us: block_forward(): chan_mean = jnp.mean(depth_out, axis=1, keepdims=True)]
    dot_general x12 -> x0, matrix products: 27.5 us -> none  [the longest x2 7.27 us: block_forward(): jnp.dot(hidden, reduce_weight, preferred_element_type=jnp.float32)]
    all_to_all x1 -> x0, waiting for transfers between devices: 16.4 us -> none  [on_device(): lax.all_to_all(packed, 'dp', split_axis=0, concat_axis=0, tiled=True)]
    all_to_all x1 -> x0, starting transfers between devices: 6.11 us -> none  [on_device(): lax.all_to_all(packed, 'dp', split_axis=0, concat_axis=0, tiled=True)]
    concatenate x2 -> x0, local copies, waits for them, and re-layouts: 6.03 us -> none  [on_device(): jnp.concatenate([expand_grad.reshape(128, 36, 128), reduce_grad.reshape(1...]
    convert_element_type x5 -> x0, other arithmetic: 3.77 us -> none  [the longest x2 3.68 us: block_forward(): normed = (unit_norm * norm_gain + norm_shift).astype(jnp.bfloat16)]
    unnamed x243 -> x38, local copies, waits for them, and re-layouts: 6.59 us -> 9.07 us
  transfers between devices with their start and end apart: 1 -> 0, of which waited for: 1 -> 0; matrix products, arithmetic and copies ran while one was open for 2% -> 0% of each run, Pallas kernels for 0% -> 0%
where the time goes in v2:
time: 114 us
  Pallas kernels  102 us (89%)
  local copies, waits for them, and re-layouts  10.3 us (9%)
  between operations  1.62 us (1%)
    pallas_call x1, Pallas kernels, forward(): pl.pallas_call(forward_kernel, out_shape=(out((PROC, 256, 384), bf16), ou...  37.9 us
    pallas_call x1, Pallas kernels, slide_step(): pl.pallas_call(slide_kernel, out_shape=(jax.ShapeDtypeStruct((1, 768), f3...  22.1 us
    pallas_call x1, Pallas kernels, reduce_scatter(): pl.pallas_call(reduce_scatter_kernel, out_shape=jax.ShapeDtypeStruct((ROW...  21.1 us
    pallas_call x1, Pallas kernels, backward(): pl.pallas_call(backward_kernel, out_shape=jax.ShapeDtypeStruct((128, 80,...  20.8 us
    unnamed x38, local copies, waits for them, and re-layouts  9.07 us

profile of v2, /device:TPU:1, one launch (start us, length us, event | category | flops | bytes accessed | tf_op | source)
XLA Modules:
  0.0 113.7 jit_solution(16699991446862571036)
XLA Ops:
  0.6 0.0 copy-start.6
  0.6 0.0 copy-start.9
  0.7 0.0 copy-start.10
  0.7 0.0 copy-start.14
  0.7 0.0 copy-start.15
  0.7 0.0 copy-start.16
  0.7 0.0 copy-start.1
  0.7 0.0 copy-start.3
  0.7 0.0 copy-start.12
  0.7 37.9 %block_forward.1 = (bf16[4,256,384]{2,1,0:T(8,128)(2,1)}, bf16[32,128]{1,0:T(8,128)(2,1)}, f32[3,2464,128]{2,1,0:T(8,128)}, f32[1024,384]{1,0:T(8,128)}, f32[102...) custom-call(s32[8,1,8]{2,1,0:T(1,128)} %routing.3, ...), custom_call_target="tpu_custom_call" | custom-call | tf_op jit(solution)/shard_map/block_forward/pallas_call | solution.py:189
  38.6 0.0 copy-start
  39.5 0.7 copy-done.11
  40.1 22.1 %slide_step.1 = (f32[1,768]{1,0:T(1,128)S(1)}, f32[48,128]{1,0:T(8,128)S(1)}) custom-call(s32[1]{0:T(128)S(6)} %copy.25.count, s32[8,1,8]{2,1,0:T(1,128)S(1)} %copy-done.10, s32[2,8]{1,0:T(2,128)S(1)} %copy-done.16, bf16[32,128]{1,0:T(8,128)(2,1)S(1)} %copy-done.11, f32[7,768]{1,0:T(8,128)S(1)} %copy-done.9, bf16[768,768]{1,0:T(8,128)(2,1)S(1)} %copy-done.6, ...), custom_call_target="tpu_custom_call" | custom-call | tf_op jit(solution)/shard_map/slide_step/pallas_call | solution.py:402
  62.3 1.9 %copy-done.2 = bf16[1024,1536]{1,0:T(8,128)(2,1)S(1)} copy-done((bf16[1024,1536]{1,0:T(8,128)(2,1)S(1)}, bf16[1024,1536]{1,0:T(8,128)(2,1)}, u32[]{:S(2)}) %copy-start.2) | copy-done | bytes 3145752
  64.2 1.4 %copy-done.4 = f32[1024,384]{1,0:T(8,128)S(1)} copy-done((f32[1024,384]{1,0:T(8,128)S(1)}, f32[1024,384]{1,0:T(8,128)}, u32[]{:S(2)}) %copy-start.4) | copy-done | bytes 1572888
  65.6 1.4 %copy-done.5 = bf16[1024,768]{1,0:T(8,128)(2,1)S(1)} copy-done((bf16[1024,768]{1,0:T(8,128)(2,1)S(1)}, bf16[1024,768]{1,0:T(8,128)(2,1)}, u32[]{:S(2)}) %copy-start.5) | copy-done | bytes 1572888
  67.0 1.1 copy-done.7
  68.1 1.0 copy-done.8
  69.2 20.8 %block_backward.1 = bf16[128,80,128]{2,1,0:T(8,128)(2,1)S(1)} custom-call(f32[48,128]{1,0:T(8,128)S(1)} %get-tuple-element.19.embed_grad, f32[3,2464,128]{2,1,0:T(8,128)} %get-tuple-element.20.cells, f32[1024,384]{1,0:T(8,128)S(1)} %copy-done.4, f32[1024,128]{1,0:T(8,128)S(1)} %copy-done.8, bf16[1024,384]{1,0:T(8,128)(2,1)S(1)} %copy-done.7, ...), custom_call_target="tpu_custom_call" | custom-call | tf_op jit(solution)/shard_map/block_backward/pallas_call | solution.py:270
  90.0 21.1 %grad_reduce_scatter.1 = f32[80,128]{1,0:T(8,128)S(1)} custom-call(bf16[4,2,4,4,80,128]{5,4,3,2,1,0:T(8,128)(2,1)S(1)} %bitcast.10), custom_call_target="tpu_custom_call" | custom-call | tf_op jit(solution)/shard_map/grad_reduce_scatter/pallas_call | solution.py:506
  111.0 0.6 slice_bitcast_fusion
  111.7 0.6 slice_bitcast_fusion.2
  112.2 0.9 copy.26
  113.1 0.6 copy.27
  (20 shorter events, 0.0 us)
Async XLA Ops:
  0.6 38.7 %copy-start.6 = (bf16[768,768]{1,0:T(8,128)(2,1)S(1)}, bf16[768,768]{1,0:T(8,128)(2,1)}, u32[]{:S(2)}) copy-start(bf16[768,768]{1,0:T(8,128)(2,1)} %weight.1) | copy-start | bytes 3538948
  0.6 38.7 %copy-start.9 = (f32[7,768]{1,0:T(8,128)S(1)}, f32[7,768]{1,0:T(8,128)}, u32[]{:S(2)}) copy-start(f32[7,768]{1,0:T(8,128)} %taps.1) | copy-start | bytes 64516
  0.7 38.7 %copy-start.10 = (s32[8,1,8]{2,1,0:T(1,128)S(1)}, s32[8,1,8]{2,1,0:T(1,128)}, u32[]{:S(2)}) copy-start(s32[8,1,8]{2,1,0:T(1,128)} %routing.3) | copy-start | bytes 772
  0.7 38.7 %copy-start.14 = (f32[768]{0:T(1024)S(1)}, f32[768]{0:T(1024)}, u32[]{:S(2)}) copy-start(f32[768]{0:T(1024)} %bias.1) | copy-start | bytes 9220
  0.7 38.7 %copy-start.15 = (f32[1,768]{1,0:T(1,128)S(1)}, f32[1,768]{1,0:T(1,128)}, u32[]{:S(2)}) copy-start(f32[1,768]{1,0:T(1,128)} %cot.1) | copy-start | bytes 9220
  0.7 38.7 %copy-start.16 = (s32[2,8]{1,0:T(2,128)S(1)}, s32[2,8]{1,0:T(2,128)}, u32[]{:S(2)}) copy-start(s32[2,8]{1,0:T(2,128)} %positions.1) | copy-start | bytes 196
  0.7 61.6 %copy-start.1 = (bf16[1536,384]{1,0:T(8,128)(2,1)S(1)}, bf16[1536,384]{1,0:T(8,128)(2,1)}, u32[]{:S(2)}) copy-start(bf16[1536,384]{1,0:T(8,128)(2,1)} %reduce.1) | copy-start | bytes 3538948
  0.7 61.6 %copy-start.3 = (bf16[384,768]{1,0:T(8,128)(2,1)S(1)}, bf16[384,768]{1,0:T(8,128)(2,1)}, u32[]{:S(2)}) copy-start(bf16[384,768]{1,0:T(8,128)(2,1)} %head.1) | copy-start | bytes 1769476
  0.7 61.6 %copy-start.12 = (f32[384]{0:T(512)S(1)}, f32[384]{0:T(512)}, u32[]{:S(2)}) copy-start(f32[384]{0:T(512)} %gain.1) | copy-start | bytes 4612
  0.7 61.6 %copy-start.13 = (f32[384]{0:T(512)S(1)}, f32[384]{0:T(512)}, u32[]{:S(2)}) copy-start(f32[384]{0:T(512)} %scale.1) | copy-start | bytes 4612
  38.6 23.7 %copy-start = (bf16[384,1536]{1,0:T(8,128)(2,1)S(1)}, bf16[384,1536]{1,0:T(8,128)(2,1)}, u32[]{:S(2)}) copy-start(bf16[384,1536]{1,0:T(8,128)(2,1)} %expand.1) | copy-start | bytes 3538948
  39.4 0.7 copy-start.11
  62.3 1.9 %copy-start.2 = (bf16[1024,1536]{1,0:T(8,128)(2,1)S(1)}, bf16[1024,1536]{1,0:T(8,128)(2,1)}, u32[]{:S(2)}) copy-start(bf16[1024,1536]{1,0:T(8,128)(2,1)} %get-tuple-element.24.hidden) | copy-start | bytes 9437188
  64.2 1.4 %copy-start.4 = (f32[1024,384]{1,0:T(8,128)S(1)}, f32[1024,384]{1,0:T(8,128)}, u32[]{:S(2)}) copy-start(f32[1024,384]{1,0:T(8,128)} %get-tuple-element.21.unit) | copy-start | bytes 4718596
  65.6 1.4 %copy-start.5 = (bf16[1024,768]{1,0:T(8,128)(2,1)S(1)}, bf16[1024,768]{1,0:T(8,128)(2,1)}, u32[]{:S(2)}) copy-start(bf16[1024,768]{1,0:T(8,128)(2,1)} %get-tuple-element.26.head_slope) | copy-start | bytes 4718596
  67.0 1.1 copy-start.7
  68.1 1.0 copy-start.8
  89.9 22.3 %copy-start.17 = (bf16[4,256,384]{2,1,0:T(8,128)(2,1)S(1)}, bf16[4,256,384]{2,1,0:T(8,128)(2,1)}, u32[]{:S(2)}) copy-start(bf16[4,256,384]{2,1,0:T(8,128)(2,1)} %get-tuple-element.16) | copy-start | bytes 2359300

commit v3 on v2

v3 whole, which is shorter than its diff:
```python
import functools
import math
import types

import jax
import jax.numpy as jnp
from jax import lax
from jax.experimental import pallas as pl
from jax.experimental.pallas import tpu as pltpu
from jax.sharding import PartitionSpec as P

PROC = 4
EPSILON = 1e-06
HALF_ROOT = 0.7071067811865476
INV_ROOT_TAU = 0.3989422804014327
MESH = pl.DeviceIdType.MESH

WIDE = 14
STEP_U = 4
ROWS_STEP = STEP_U * 64
CHUNK = STEP_U * 16


def nt_dot(left, right):
    return lax.dot_general(left, right, (((1,), (1,)), ((), ())), preferred_element_type=jnp.float32)


def tn_dot(left, right):
    return lax.dot_general(left, right, (((0,), (0,)), ((), ())), preferred_element_type=jnp.float32)


def gelu_and_slope(pre):
    phi = 0.5 + 0.5 * lax.erf(pre * HALF_ROOT)
    return pre * phi, phi + pre * (INV_ROOT_TAU * jnp.exp(-0.5 * (pre * pre)))


def tile_sources(routing, dp):
    source = []
    for q in range(PROC):
        found = -1
        for d in range(8):
            for s in range(8):
                found = jnp.where(routing[d, 0, s] == dp * PROC + q, d, found)
        source.append(found)
    return source


def emit_tiles(ref, source):
    def tile_row(u, carry):
        for q in range(PROC):
            for block in range(3):
                left = ref.section[block, pl.ds(u * 64 + q * 2, 8, stride=8), :]
                right = ref.section[block, pl.ds(u * 64 + q * 2 + 1, 8, stride=8), :]
                row = jnp.where(source[q] >= 0, jnp.concatenate([left, right], axis=0), 0.0)
                ref.tile_out[q, pl.ds(pl.multiple_of(u * 16, 16), 16), pl.ds(block * 128, 128)] = row.astype(jnp.bfloat16)
        return carry

    lax.fori_loop(0, 16, tile_row, 0)


def forward(ref, dp, group):
    f32, bf16 = jnp.float32, jnp.bfloat16
    routing, tiles, leaving, send, recv = ref.routing, ref.tiles, ref.leaving, ref.tile_send, ref.tile_recv
    cells, section, embed_sum, depth = ref.cells, ref.section, ref.embed_sum, ref.depth
    peers = [lax.rem(dp + k, 8) for k in range(8)]

    def slot_for(to):
        found = 0
        for s in range(1, 8):
            local = routing[dp, 0, s] - to * PROC
            found = jnp.where((local >= 0) & (local < PROC), s, found)
        return found

    slots = [slot_for(to) for to in peers]
    source = tile_sources(routing, dp)

    arrived = (ref.arrived0, ref.arrived1, ref.arrived2, ref.arrived3)

    def chunk_copy(c, k):
        return pltpu.make_async_remote_copy(
            src_ref=leaving.at[k - 1, pl.ds(c * CHUNK, CHUNK)], dst_ref=arrived[c].at[dp], send_sem=send.at[c * 7 + k - 1],
            recv_sem=recv.at[c * 7 + k - 1], device_id=(peers[k], group), device_id_type=MESH)

    pl.semaphore_wait(pltpu.get_barrier_semaphore(), 22)
    ref.fetches[0].wait()

    for c in range(4):
        rows = pl.ds(c * CHUNK, CHUNK)
        for k in (4, 5, 3, 2, 6, 1, 7):
            leaving[k - 1, rows, :] = tiles[slots[k], rows, :]
            chunk_copy(c, k).start()
        arrived[c][dp] = tiles[slots[0], rows, :]
    edge = 3 * WIDE * 8
    cells[:, 0:edge] = jnp.zeros((3, edge, 128), f32)
    cells[:, edge + 16 * WIDE * 8:] = jnp.zeros((3, edge, 128), f32)
    zeros3 = jnp.zeros((3, 128), f32)

    def fill(c, i):
        u = c * STEP_U + i
        base = (u + 3) * (WIDE * 8)
        for q in range(PROC):
            src = source[q]
            row = arrived[c][jnp.maximum(src, 0), i * 16:i * 16 + 16, :].astype(f32)
            row = jnp.where(src >= 0, row, 0.0)
            for block in range(3):
                lanes = slice(block * 128, block * 128 + 128)
                cells[block, pl.ds(base + q * 2, 3, stride=8), :] = zeros3
                cells[block, pl.ds(base + 24 + q * 2, 11, stride=8), :] = row[0:11, lanes]
                cells[block, pl.ds(base + q * 2 + 1, 11, stride=8), :] = row[5:16, lanes]
                cells[block, pl.ds(base + 88 + q * 2 + 1, 3, stride=8), :] = zeros3

    def land(c):
        for k in range(1, 8):
            chunk_copy(c, k).wait_recv()
        for i in range(STEP_U):
            fill(c, i)

    for copy in ref.fetches[1:]:
        copy.wait()
    land(0)
    embed_sum[...] = jnp.zeros((6, 8, 128), f32)

    def step(n, carry):
        start = pl.multiple_of(n * ROWS_STEP, ROWS_STEP)

        for c in range(1, 4):
            @pl.when(n == c - 1)
            def _():
                land(c)

        for block in range(3):
            lanes = pl.ds(block * 128, 128)
            for part in range(STEP_U // 2):
                acc = [jnp.zeros((8, 8, 128), f32) + ref.depth_bias[lanes].reshape(1, 1, 128) for _ in range(2)]
                for a in range(8):
                    first = pl.multiple_of((n * STEP_U + part * 2 + a) * (WIDE * 8), 8)
                    x = cells[block, pl.ds(first, WIDE * 8), :].reshape(WIDE, 8, 128)
                    for i in range(2):
                        if 0 <= a - i < 7:
                            for b in range(7):
                                acc[i] = acc[i] + ref.depth_kernel[pl.ds((a - i) * 7 + b, 1), lanes].reshape(1, 1, 128) * x[b:b + 8]
                for i in range(2):
                    depth[pl.ds((part * 2 + i) * 64, 64), lanes] = acc[i].reshape(64, 128)
        value = depth[...]
        centred = value - jnp.mean(value, axis=1, keepdims=True)
        inv = lax.rsqrt(jnp.mean(centred * centred, axis=1, keepdims=True) + EPSILON)
        z = centred * inv
        ref.unit[pl.ds(start, ROWS_STEP), :] = z
        ref.inv_std[pl.ds(start, ROWS_STEP), :] = jnp.broadcast_to(inv, (ROWS_STEP, 128))
        norm = (z * ref.gain[...].reshape(1, 384) + ref.shift[...].reshape(1, 384)).astype(bf16)
        ref.normed[pl.ds(start, ROWS_STEP), :] = norm
        for m in range(6):
            cols = pl.ds(m * 256, 256)
            pre = jnp.dot(norm, ref.expand[:, cols], preferred_element_type=f32) + ref.expand_bias[cols].reshape(1, 256)
            act, grad = gelu_and_slope(pre)
            ref.hidden[pl.ds(start, ROWS_STEP), cols] = act.astype(bf16)
            ref.slope[pl.ds(start, ROWS_STEP), cols] = grad.astype(bf16)
        mlp = jnp.dot(ref.hidden[pl.ds(start, ROWS_STEP), :], ref.reduce[...], preferred_element_type=f32) + ref.reduce_bias[...].reshape(1, 384)
        mlp = mlp * ref.scale[...].reshape(1, 384)
        for i in range(STEP_U):
            first = pl.multiple_of((n * STEP_U + i + 3) * (WIDE * 8) + 24, 8)
            for block in range(3):
                section[block, pl.ds(pl.multiple_of(start + i * 64, 64), 64), :] = cells[block, pl.ds(first, 64), :] + mlp[i * 64:(i + 1) * 64, block * 128:block * 128 + 128]
        sec = jnp.concatenate([section[block, pl.ds(start, ROWS_STEP), :] for block in range(3)], axis=1).astype(bf16)
        for m in range(3):
            cols = pl.ds(m * 256, 256)
            act, grad = gelu_and_slope(jnp.dot(sec, ref.head[:, cols], preferred_element_type=f32))
            ref.head_slope[pl.ds(start, ROWS_STEP), cols] = grad.astype(bf16)
            act = jnp.sum(act.reshape(STEP_U * 8, 8, 256), axis=0)
            for half in range(2):
                embed_sum[m * 2 + half] = embed_sum[m * 2 + half] + act[:, half * 128:half * 128 + 128]
        return carry

    lax.fori_loop(0, 16 // STEP_U, step, 0)
    means = [
        (embed_sum[block, pl.ds(0, 4, stride=2), :] + embed_sum[block, pl.ds(1, 4, stride=2), :]) * (1.0 / 256.0)
        for block in range(6)
    ]
    ref.embed[...] = jnp.concatenate(means + [jnp.zeros((8, 128), f32)], axis=0).astype(bf16)

    def departed():
        for c in range(4):
            for k in range(1, 8):
                chunk_copy(c, k).wait_send()

    return departed


def slide_pass(ref, dp, group):
    routing, emb_all, rows_mine, rows_all = ref.routing, ref.emb_all, ref.rows_mine, ref.rows_all
    wide, grad_wide, grad_mine, grad_all = ref.wide, ref.grad_wide, ref.grad_mine, ref.grad_all
    f32, bf16, i32 = jnp.float32, jnp.bfloat16, jnp.int32
    dp_peers = [lax.rem(dp + k, 8) for k in range(1, 8)]
    group_peers = [lax.rem(group + k, 16) for k in range(1, 16)]

    def over_dp(source, landing, send, recv):
        copies = []
        for k, to in enumerate(dp_peers):
            cp = pltpu.make_async_remote_copy(src_ref=source, dst_ref=landing.at[dp], send_sem=send.at[k], recv_sem=recv.at[k], device_id=(to, group), device_id_type=MESH)
            cp.start()
            copies.append(cp)
        landing[dp] = source[...]
        return copies

    def iota(shape, axis):
        return lax.broadcasted_iota(i32, shape, axis)

    copies1 = over_dp(ref.embed, emb_all, ref.slide_send1, ref.slide_recv1)
    places = ref.count[0]

    row = iota((48, 128), 0)
    slot, block = row & 7, row >> 3
    channel = jnp.where(block >= 3, block - 3, block) * 128 + iota((48, 128), 1)
    spot = jnp.zeros((48, 128), i32)
    for s in range(8):
        spot = jnp.where(slot == s, jnp.where(block >= 3, ref.positions[1, s], ref.positions[0, s]), spot)
    frequency = jnp.exp((channel - (channel & 1)).astype(f32) * (-math.log(10000.0) / 384))
    angle = spot.astype(f32) * frequency
    pos_code = jnp.where((channel & 1) == 0, jnp.sin(angle), jnp.cos(angle))
    here = slot * 16 + group < places

    pick_row, pick_col = iota((48, 32), 0), iota((48, 32), 1)
    goes_to = jnp.full((48, 32), -1, i32)
    for s in range(8):
        goes_to = jnp.where((pick_row & 7) == s, routing[dp, 0, s], goes_to)
    goes_to = jnp.where((pick_row >> 3) == (pick_col >> 2), goes_to, -1)
    grad_row, grad_col = iota((48, 48), 0), iota((48, 48), 1)
    grad_place = jnp.where((grad_row >> 3) == (grad_col >> 3), dp * PROC + ((grad_row & 7) >> 1), -2)
    grad_picks = []
    for d in range(8):
        routed = jnp.full((48, 48), -1, i32)
        for s in range(8):
            routed = jnp.where((grad_col & 7) == s, routing[d, 0, s], routed)
        grad_picks.append(jnp.where(routed == grad_place, 1.0, 0.0).astype(bf16))

    emit_tiles(ref, tile_sources(routing, dp))
    for cp in copies1:
        cp.wait_recv()
    own = pos_code
    for e in range(8):
        pick = jnp.where(goes_to == e * PROC + (pick_col & 3), 1.0, 0.0).astype(bf16)
        own = own + jnp.dot(pick, emb_all[e], preferred_element_type=f32)
    rows_mine[...] = jnp.where(here, own, 0.0).astype(bf16)
    copies2 = []
    for k, to in enumerate(group_peers):
        cp = pltpu.make_async_remote_copy(src_ref=rows_mine, dst_ref=rows_all.at[group], send_sem=ref.slide_send2.at[k], recv_sem=ref.slide_recv2.at[k], device_id=(dp, to), device_id_type=MESH)
        cp.start()
        copies2.append(cp)
    rows_all[group] = rows_mine[...]
    for cp in copies2:
        cp.wait_recv()

    first, last = slot[0:8] == 0, slot[0:8] == 7

    def widen(block_rows, target):
        target[9:25] = block_rows
        for g in range(9):
            target[g] = jnp.where(first, 0.0, pltpu.roll(block_rows[g + 7], 1, 0))
            target[25 + g] = jnp.where(last, 0.0, pltpu.roll(block_rows[g], 7, 0))

    mixed = []
    for b in range(6):
        rows = rows_all[:, b * 8:b * 8 + 8, :].astype(f32)
        widen(rows, wide)
        total = rows
        for k in range(7):
            total = total + ref.slide_taps[pl.ds(k, 1), pl.ds(b * 128, 128)].reshape(1, 1, 128) * wide[3 * k:3 * k + 16]
        mixed.append(total.reshape(128, 128).astype(bf16))
    mixed = jnp.concatenate(mixed, axis=1)
    pre = jnp.dot(mixed, ref.slide_weight[...], preferred_element_type=f32) + ref.slide_bias[...].reshape(1, 768)
    seq_row = iota((128, 768), 0)
    share = jnp.where((seq_row & 7) * 16 + (seq_row >> 3) < places, 1.0, 0.0) / places.astype(f32)
    phi = 0.5 * (1.0 + lax.erf(pre * HALF_ROOT))
    slope = phi + pre * INV_ROOT_TAU * jnp.exp(-0.5 * pre * pre)
    grad_agg = (ref.cot[...] * share * slope).astype(bf16)
    grad_mixed = lax.dot_general(grad_agg, ref.slide_weight[...], (((1,), (1,)), ((), ())), preferred_element_type=f32)
    grad_rows = []
    for b in range(6):
        widen(grad_mixed[:, b * 128:b * 128 + 128].reshape(16, 8, 128), grad_wide)
        total = grad_wide[9 + group]
        for k in range(7):
            total = total + ref.slide_taps[pl.ds(k, 1), pl.ds(b * 128, 128)] * grad_wide[group + 18 - 3 * k]
        grad_rows.append(total)
    grad_mine[...] = jnp.where(here, jnp.concatenate(grad_rows, axis=0), 0.0).astype(bf16)
    copies3 = over_dp(grad_mine, grad_all, ref.slide_send3, ref.slide_recv3)
    ref.feature[...] = jnp.sum(pre * phi * share, axis=0, keepdims=True)
    for cp in copies3:
        cp.wait_recv()
    total = jnp.zeros((48, 128), f32)
    for d in range(8):
        total = total + jnp.dot(grad_picks[d], grad_all[d], preferred_element_type=f32)
    ref.embed_grad[...] = total
    return copies1 + copies2 + copies3


def backward_weights(ref):
    f32, bf16 = jnp.float32, jnp.bfloat16
    eg_row = jnp.concatenate([ref.embed_grad[8 * block:8 * block + 8] for block in range(6)], axis=1) * (1.0 / 256.0)

    def first(n, carry):
        rows = pl.ds(pl.multiple_of(n * 256, 256), 256)
        gh = (eg_row[None] * ref.head_slope[rows, :].astype(f32).reshape(32, 8, 768)).reshape(256, 768).astype(bf16)
        ref.grad_mlp[rows, :] = (ref.scale[...].reshape(1, 384) * nt_dot(gh, ref.head[...])).astype(bf16)
        return carry

    lax.fori_loop(0, 4, first, 0)

    for m in range(6):
        cols = pl.ds(m * 256, 256)
        for n in range(4):
            rows = pl.ds(n * 256, 256)
            gp = nt_dot(ref.grad_mlp[rows, :], ref.reduce[cols, :]) * ref.slope[rows, cols].astype(f32)
            ref.grad_pre[rows, cols] = gp.astype(bf16)
        eg_m = tn_dot(ref.normed[...], ref.grad_pre[:, cols])
        for l in range(2):
            ref.flat[pl.ds(m * 2 + l, 384, stride=12), :] = eg_m[:, l * 128:(l + 1) * 128]
    for m in range(6):
        rg_m = tn_dot(ref.hidden[:, pl.ds(m * 256, 256)], ref.grad_mlp[...])
        for l in range(3):
            ref.flat2[pl.ds(m * 768 + l, 256, stride=3), :] = rg_m[:, l * 128:(l + 1) * 128]

    ref.flat2[4608:] = jnp.zeros((8, 128), f32)

    def pack(i, carry):
        ref.shares[i, 0:32] = ref.flat[pl.ds(i * 36, 32), :].astype(bf16)
        ref.shares[i, 32:48] = jnp.concatenate(
            [ref.flat[pl.ds(i * 36 + 32, 4), :], jnp.zeros((4, 128), f32), ref.flat2[pl.ds(i * 36, 8), :]], axis=0
        ).astype(bf16)
        ref.shares[i, 48:80] = ref.flat2[pl.ds(i * 36 + 8, 32), :].astype(bf16)
        return carry

    lax.fori_loop(0, 128, pack, 0)


def backward_norm(ref):
    f32, bf16 = jnp.float32, jnp.bfloat16

    def second(n, carry):
        rows = pl.ds(pl.multiple_of(n * 256, 256), 256)
        w = nt_dot(ref.grad_pre[rows, :], ref.expand[...]) * ref.gain[...].reshape(1, 384)
        z = ref.unit[rows, :]
        inv = jnp.concatenate([ref.inv_std[rows, :]] * 3, axis=1)
        ref.depthwise[rows, :] = inv * (w - jnp.mean(w, axis=1, keepdims=True) - z * jnp.mean(w * z, axis=1, keepdims=True))
        return carry

    lax.fori_loop(0, 4, second, 0)


def backward_depth(ref):
    f32 = jnp.float32
    ref.taps[147:] = jnp.zeros((21, 128), f32)
    for block in range(3):
        lanes = pl.ds(block * 128, 128)
        for a in range(7):
            def row(u, acc):
                g = ref.depthwise[pl.ds(pl.multiple_of(u * 64, 64), 64), lanes].reshape(8, 8, 128)
                x = ref.cells[block, pl.ds(pl.multiple_of((u + a) * (WIDE * 8), 8), WIDE * 8), :].reshape(WIDE, 8, 128)
                return tuple(acc[b] + jnp.sum(g * x[b:b + 8], axis=0) for b in range(7))
            acc = lax.fori_loop(0, 16, row, tuple(jnp.zeros((8, 128), f32) for _ in range(7)))
            for b in range(7):
                ref.taps[pl.ds((a * 7 + b) * 3 + block, 1), :] = jnp.sum(acc[b], axis=0, keepdims=True)


def depth_exchange(ref, dp, group):
    f32, bf16 = jnp.float32, jnp.bfloat16
    copies = []
    for k in range(1, 8):
        to = lax.rem(dp + k, 8)
        ref.tap_leaving[k - 1] = ref.taps[pl.ds(lax.div(147 * to, 8), 32), :].astype(bf16)
        cp = pltpu.make_async_remote_copy(src_ref=ref.tap_leaving.at[k - 1], dst_ref=ref.tap_arrived.at[k - 1], send_sem=ref.tap_send.at[k - 1], recv_sem=ref.tap_recv.at[k - 1], device_id=(to, group), device_id_type=MESH)
        cp.start()
        copies.append(cp)
    yield
    total = ref.taps[pl.ds(lax.div(147 * dp, 8), 32), :]
    for cp in copies:
        cp.wait_recv()
    for k in range(7):
        total = total + ref.tap_arrived[k].astype(f32)
    ref.tap_mine[...] = total.astype(bf16)
    for k in range(1, 16):
        to = lax.rem(group + k, 16)
        cp = pltpu.make_async_remote_copy(src_ref=ref.tap_mine, dst_ref=ref.tap_group.at[k - 1], send_sem=ref.tap_send.at[6 + k], recv_sem=ref.tap_recv.at[6 + k], device_id=(dp, to), device_id_type=MESH)
        cp.start()
        copies.append(cp)
    yield
    for cp in copies[7:]:
        cp.wait_recv()
    for k in range(15):
        total = total + ref.tap_group[k].astype(f32)
    ref.tap_sum[...] = total
    begin = 147 * (16 * dp + group)
    row = lax.div(begin, 128) - lax.div(147 * dp, 8)
    turn = lax.rem(begin, 128)
    near = pltpu.roll(ref.tap_sum[pl.ds(row, 8), :], 128 - turn, 1)
    lane = lax.broadcasted_iota(jnp.int32, (8, 128), 1)
    ref.depth_out[...] = jnp.where(lane < 128 - turn, near, pltpu.roll(near, 7, 0))
    for cp in copies:
        cp.wait_send()


PARTS = (32, 32, 16)
ORDERS = ("yxz", "xzy", "zyx")
ROWS = sum(PARTS)

def torus_place():
    dp, group = lax.axis_index("dp"), lax.axis_index("group")
    return {"y": lax.div(dp, 2), "c": lax.rem(dp, 2), "x": lax.div(group, 4), "z": lax.rem(group, 4)}

def torus_device(place, **moved):
    at = {**place, **moved}
    return (at["y"] * 2 + at["c"], at["x"] * 4 + at["z"])

def share_exchange(ref):
    place = torus_place()
    partner = torus_device(place, c=1 - place["c"])
    core_in, core_send, core_recv, send, recv = ref.core_in, ref.core_send, ref.core_recv, ref.share_send, ref.share_recv
    s1, s2, s3, r1, r2, r3 = ref.s1, ref.s2, ref.s3, ref.r1, ref.r2, ref.r3
    core_copies = []
    for y in range(4):
        cp = pltpu.make_async_remote_copy(src_ref=ref.shares.at[pl.ds(pl.multiple_of((y * 2 + 1 - place["c"]) * 16, 16), 16)], dst_ref=core_in.at[y], send_sem=core_send.at[y], recv_sem=core_recv.at[y], device_id=partner, device_id_type=MESH)
        cp.start()
        core_copies.append(cp)

    def start(stage, part, source, landing):
        axis = ORDERS[part][stage]
        made = []
        for k in (2, 1, 3):
            to = lax.rem(place[axis] + k, 4)
            cp = pltpu.make_async_remote_copy(src_ref=source.at[to], dst_ref=landing.at[k - 1], send_sem=send.at[stage * 9 + part * 3 + k - 1], recv_sem=recv.at[stage * 9 + part * 3 + k - 1], device_id=torus_device(place, **{axis: to}), device_id_type=MESH)
            cp.start()
            made.append(cp)
        return made

    yield
    f32 = jnp.float32
    for y in range(4):
        core_copies[y].wait_recv()
        for x in range(4):
            both = ref.shares[pl.ds((y * 2 + place["c"]) * 16 + x * 4, 4)].astype(f32) + core_in[y, x * 4:x * 4 + 4].astype(f32)
            both = both.astype(jnp.bfloat16)
            s1[0][y, x] = both[:, 0:32]
            s1[1][x, :, y] = both[:, 32:64]
            for z in range(4):
                s1[2][z, y, x] = both[z, 64:80]
    flying = [start(0, part, s1[part], r1[part]) for part in range(3)]
    yield
    flying2 = []
    for part in range(3):
        for cp in flying[part]:
            cp.wait_recv()
        mine = place[ORDERS[part][0]]
        for a in range(4):
            total = s1[part][mine, a].astype(f32)
            for k in range(3):
                total = total + r1[part][k, a].astype(f32)
            s2[part][a] = total.astype(jnp.bfloat16)
        flying2.append(start(1, part, s2[part], r2[part]))
    yield
    flying3 = []
    for part in range(3):
        for cp in flying2[part]:
            cp.wait_recv()
        mine = place[ORDERS[part][1]]
        total = s2[part][mine].astype(f32)
        for k in range(3):
            total = total + r2[part][k].astype(f32)
        s3[part][...] = total.astype(jnp.bfloat16)
        flying3.append(start(2, part, s3[part], r3[part]))
    yield
    base = 0
    for part in range(3):
        for cp in flying3[part]:
            cp.wait_recv()
        total = s3[part][place[ORDERS[part][2]]].astype(f32)
        for k in range(3):
            total = total + r3[part][k].astype(f32)
        ref.share_sum[base:base + PARTS[part]] = total
        base += PARTS[part]
    ref.expand_out[...] = ref.share_sum[0:36]
    ref.reduce_out[...] = ref.share_sum[40:76]
    for cp in core_copies:
        cp.wait_send()
    for copies in flying + flying2 + flying3:
        for cp in copies:
            cp.wait_send()


SCALARS = ("count", "routing", "positions")
FETCHED = ("tiles", "depth_kernel", "depth_bias", "gain", "shift", "expand", "expand_bias", "reduce", "reduce_bias",
           "scale", "head", "slide_taps", "slide_weight", "slide_bias", "cot")
RESULTS = ("tile_out", "feature", "expand_out", "reduce_out", "depth_out")


def scratch_list(arrays):
    f32, bf16 = jnp.float32, jnp.bfloat16
    vm = pltpu.VMEM
    sem = lambda n: pltpu.SemaphoreType.DMA((n,))
    parts = lambda *lead: [vm(lead + (rows, 128), bf16) for rows in PARTS]
    held = {name: vm(a.shape, a.dtype) for name, a in zip(FETCHED, arrays)}
    return {
        **held,
        "fetch_sem": sem(len(FETCHED)),
        "leaving": vm((7, 256, 384), bf16),
        **{f"arrived{c}": vm((8, CHUNK, 384), bf16) for c in range(4)},
        "tile_send": sem(28), "tile_recv": sem(28),
        "cells": vm((3, 22 * WIDE * 8, 128), f32),
        "unit": vm((1024, 384), f32), "inv_std": vm((1024, 128), f32), "normed": vm((1024, 384), bf16),
        "hidden": vm((1024, 1536), bf16), "slope": vm((1024, 1536), bf16), "head_slope": vm((1024, 768), bf16),
        "depth": vm((ROWS_STEP, 384), f32), "section": vm((3, 1024, 128), f32), "embed_sum": vm((6, 8, 128), f32),
        "embed": vm((32, 128), bf16),
        "emb_all": vm((8, 32, 128), bf16), "rows_mine": vm((48, 128), bf16), "rows_all": vm((16, 48, 128), bf16),
        "wide": vm((34, 8, 128), f32), "grad_wide": vm((34, 8, 128), f32),
        "grad_mine": vm((48, 128), bf16), "grad_all": vm((8, 48, 128), bf16), "embed_grad": vm((48, 128), f32),
        "slide_send1": sem(7), "slide_recv1": sem(7), "slide_send2": sem(15), "slide_recv2": sem(15),
        "slide_send3": sem(7), "slide_recv3": sem(7),
        "grad_mlp": vm((1024, 384), bf16), "grad_pre": vm((1024, 1536), bf16), "depthwise": vm((1024, 384), f32),
        "flat": vm((4608, 128), f32), "flat2": vm((4616, 128), f32), "shares": vm((128, ROWS, 128), bf16),
        "taps": vm((168, 128), f32),
        "core_in": vm((4, 16, ROWS, 128), bf16),
        "s1": parts(4, 4, 4), "s2": parts(4, 4), "s3": parts(4),
        "r1": parts(3, 4, 4), "r2": parts(3, 4), "r3": parts(3),
        "core_send": sem(4), "core_recv": sem(4), "share_send": sem(27), "share_recv": sem(27),
        "share_sum": vm((ROWS, 128), f32),
        "tap_leaving": vm((7, 32, 128), bf16), "tap_arrived": vm((7, 32, 128), bf16), "tap_mine": vm((32, 128), bf16),
        "tap_group": vm((15, 32, 128), bf16), "tap_sum": vm((32, 128), f32), "tap_send": sem(22), "tap_recv": sem(22),
    }


def step_kernel(names, *refs):
    count = len(SCALARS) + len(FETCHED)
    ref = types.SimpleNamespace(**dict(zip(SCALARS, refs)))
    sources = refs[len(SCALARS):count]
    for name, one in zip(RESULTS, refs[count:]):
        setattr(ref, name, one)
    for name, one in zip(names, refs[count + len(RESULTS):]):
        setattr(ref, name, one)
    ref.fetches = [
        pltpu.make_async_copy(source, getattr(ref, name), ref.fetch_sem.at[i])
        for i, (name, source) in enumerate(zip(FETCHED, sources))
    ]
    for copy in ref.fetches:
        copy.start()
    dp, group = lax.axis_index("dp"), lax.axis_index("group")
    barrier = pltpu.get_barrier_semaphore()
    for k in range(1, 8):
        pl.semaphore_signal(barrier, inc=1, device_id=(lax.rem(dp + k, 8), group), device_id_type=MESH)
    for k in range(1, 16):
        pl.semaphore_signal(barrier, inc=1, device_id=(dp, lax.rem(group + k, 16)), device_id_type=MESH)
    departed = forward(ref, dp, group)
    copies = slide_pass(ref, dp, group)
    backward_weights(ref)
    shares = share_exchange(ref)
    next(shares)
    backward_norm(ref)
    next(shares)
    backward_depth(ref)
    taps = depth_exchange(ref, dp, group)
    next(taps)
    next(shares)
    next(taps)
    next(shares)
    for rest in (taps, shares):
        for _ in rest:
            pass
    for cp in copies:
        cp.wait_send()
    departed()


def training_step(*arrays):
    f32 = jnp.float32
    vm = pl.BlockSpec(memory_space=pltpu.VMEM)
    scratch = scratch_list(arrays[len(SCALARS):])
    out = jax.ShapeDtypeStruct
    return pl.pallas_call(
        functools.partial(step_kernel, tuple(scratch)),
        out_shape=(out((PROC, 256, 384), jnp.bfloat16), out((1, 768), f32), out((36, 128), f32), out((36, 128), f32),
                   out((8, 128), f32)),
        in_specs=[pl.BlockSpec(memory_space=pltpu.SMEM)] * len(SCALARS)
        + [pl.BlockSpec(memory_space=pl.ANY)] * len(FETCHED),
        out_specs=(vm,) * len(RESULTS),
        scratch_shapes=list(scratch.values()),
        compiler_params=pltpu.CompilerParams(collective_id=1, has_side_effects=True, vmem_limit_bytes=60 * 2**20),
        name="training_step",
    )(*arrays)


def on_device(
    tile_maps,
    positions,
    counts,
    routing,
    depth_kernel,
    depth_bias,
    norm_gain,
    norm_shift,
    expand_weight,
    expand_bias,
    reduce_weight,
    reduce_bias,
    layer_scale,
    head_weight,
    slide_taps,
    slide_weight,
    slide_bias,
    cotangent,
):
    tile_out, feature, expand_share, reduce_share, depth_share = training_step(
        counts,
        routing,
        positions,
        tile_maps.reshape(8, 256, 384),
        depth_kernel,
        depth_bias,
        norm_gain,
        norm_shift,
        expand_weight,
        expand_bias,
        reduce_weight,
        reduce_bias,
        layer_scale,
        head_weight,
        slide_taps,
        slide_weight,
        slide_bias,
        cotangent,
    )
    return (
        tile_out.reshape((PROC,) + tile_maps.shape[1:]),
        feature,
        expand_share.reshape(-1),
        reduce_share.reshape(-1),
        depth_share[:2].reshape(-1)[:147],
    )


def solution(mesh):
    return jax.shard_map(
        on_device,
        mesh=mesh,
        in_specs=(
            P(("dp", "group"), None, None, None),
            P(None, ("dp", "group")),
            P("dp"),
            P(None, "group", None),
            P(),
            P(),
            P(),
            P(),
            P(),
            P(),
            P(),
            P(),
            P(),
            P(),
            P(),
            P(),
            P(),
            P("dp", None),
        ),
        out_specs=(
            P(("dp", "group"), None, None, None),
            P("dp", None),
            P(("dp", "group")),
            P(("dp", "group")),
            P(("dp", "group")),
        ),
        check_vma=False,
    )
```

time: 114 us -> 87.8 us (0.77)
  Pallas kernels: 102 us -> 81.1 us
  local copies, waits for them, and re-layouts: 10.3 us -> 5.14 us
    pallas_call x4 -> x1, Pallas kernels: 102 us -> 81.1 us  [training_step(): pl.pallas_call(functools.partial(step_kernel, tuple(scratch)), out_shape=...]
    unnamed x38 -> x10, local copies, waits for them, and re-layouts: 9.07 us -> 3.9 us
where the time goes in v3:
time: 87.8 us; the launch traced here: 87.5 us
  Pallas kernels  81.1 us (92%)
  local copies, waits for them, and re-layouts  5.14 us (6%)
  between operations  1.32 us (2%)
    pallas_call x1, Pallas kernels, training_step(): pl.pallas_call(functools.partial(step_kernel, tuple(scratch)), out_shape=...  81.1 us
    unnamed x10, local copies, waits for them, and re-layouts  3.9 us

profile of v3, /device:TPU:1, one launch (start us, length us, event | category | flops | bytes accessed | tf_op | source)
XLA Modules:
  0.0 87.5 jit_solution(5784845442263596900)
XLA Ops:
  1.3 81.1 %training_step.1 = (bf16[4,256,384]{2,1,0:T(8,128)(2,1)}, f32[1,768]{1,0:T(1,128)}, f32[36,128]{1,0:T(8,128)}, f32[36,128]{1,0:T(8,128)}, f32[8,128]{1,0:T(8,128)}) custom-call(s32[1]{0:T(128)S(6)} %copy.27.refs_0_, s32[8,1,8]{2,1,0:T(1,128)} %refs_1_.1, s32[2,8]{1,0:T(2,128)} %refs_2_.1, bf16[8,256,384]{2,1,0:T(8,128)(2,1)} %bitcast.7, f32[49,384]{1,0:T(8,128)} %refs_4_.1, ...), custom_call_target="tpu_custom_call" | custom-call | tf_op jit(solution)/shard_map/training_step/pallas_call | solution.py:575
  82.4 0.0 copy-start.2
  82.4 0.0 copy-start.1
  82.4 0.0 copy-start
  82.4 1.2 %slice_bitcast_fusion = f32[256]{0:T(256)} fusion(f32[8,128]{1,0:T(8,128)} %get-tuple-element.14), kind=kLoop, calls=%fused_computation | loop fusion | bytes 2048 | tf_op jit(solution)/shard_map/reshape | solution.py:633
  83.6 2.1 %copy.28 = bf16[4,16,16,384]{3,2,1,0:T(8,128)(2,1)} copy(bf16[4,16,16,384]{3,2,1,0:T(8,128)(2,1)} %bitcast.8) | data formatting | bytes 1572864
  85.7 0.0 copy-done.2
  85.7 0.6 copy.29
  86.3 0.0 copy-done.1
  86.3 0.6 copy.30
  86.9 0.0 copy-done
  86.9 0.6 copy.31
Async XLA Ops:
  82.4 3.4 %copy-start.2 = (f32[1,768]{1,0:T(1,128)S(1)}, f32[1,768]{1,0:T(1,128)}, u32[]{:S(2)}) copy-start(f32[1,768]{1,0:T(1,128)} %get-tuple-element.21) | copy-start | bytes 9220
  82.4 3.9 %copy-start.1 = (f32[36,128]{1,0:T(8,128)S(1)}, f32[36,128]{1,0:T(8,128)}, u32[]{:S(2)}) copy-start(f32[36,128]{1,0:T(8,128)} %get-tuple-element.12) | copy-start | bytes 55300
  82.4 4.5 %copy-start = (f32[36,128]{1,0:T(8,128)S(1)}, f32[36,128]{1,0:T(8,128)}, u32[]{:S(2)}) copy-start(f32[36,128]{1,0:T(8,128)} %get-tuple-element.13) | copy-start | bytes 55300

commit v4 on v3

--- a/solution.py
+++ b/solution.py
@@ -18,7 +18,8 @@
 WIDE = 14
 STEP_U = 4
 ROWS_STEP = STEP_U * 64
-CHUNK = STEP_U * 16
+CHUNKS = (7, 4, 4, 1)
+CHUNK_AT = (0, 7, 11, 15)
 
 
 def nt_dot(left, right):
@@ -78,14 +79,14 @@
 
     def chunk_copy(c, k):
         return pltpu.make_async_remote_copy(
-            src_ref=leaving.at[k - 1, pl.ds(c * CHUNK, CHUNK)], dst_ref=arrived[c].at[dp], send_sem=send.at[c * 7 + k - 1],
+            src_ref=leaving.at[k - 1, pl.ds(CHUNK_AT[c] * 16, CHUNKS[c] * 16)], dst_ref=arrived[c].at[dp], send_sem=send.at[c * 7 + k - 1],
             recv_sem=recv.at[c * 7 + k - 1], device_id=(peers[k], group), device_id_type=MESH)
 
     pl.semaphore_wait(pltpu.get_barrier_semaphore(), 22)
     ref.fetches[0].wait()
 
     for c in range(4):
-        rows = pl.ds(c * CHUNK, CHUNK)
+        rows = pl.ds(CHUNK_AT[c] * 16, CHUNKS[c] * 16)
         for k in (4, 5, 3, 2, 6, 1, 7):
             leaving[k - 1, rows, :] = tiles[slots[k], rows, :]
             chunk_copy(c, k).start()
@@ -96,7 +97,7 @@
     zeros3 = jnp.zeros((3, 128), f32)
 
     def fill(c, i):
-        u = c * STEP_U + i
+        u = CHUNK_AT[c] + i
         base = (u + 3) * (WIDE * 8)
         for q in range(PROC):
             src = source[q]
@@ -112,7 +113,7 @@
     def land(c):
         for k in range(1, 8):
             chunk_copy(c, k).wait_recv()
-        for i in range(STEP_U):
+        for i in range(CHUNKS[c]):
             fill(c, i)
 
     for copy in ref.fetches[1:]:
@@ -124,7 +125,7 @@
         start = pl.multiple_of(n * ROWS_STEP, ROWS_STEP)
 
         for c in range(1, 4):
-            @pl.when(n == c - 1)
+            @pl.when(n == c)
             def _():
                 land(c)
 
@@ -501,7 +502,7 @@
         **held,
         "fetch_sem": sem(len(FETCHED)),
         "leaving": vm((7, 256, 384), bf16),
-        **{f"arrived{c}": vm((8, CHUNK, 384), bf16) for c in range(4)},
+        **{f"arrived{c}": vm((8, rows * 16, 384), bf16) for c, rows in enumerate(CHUNKS)},
         "tile_send": sem(28), "tile_recv": sem(28),
         "cells": vm((3, 22 * WIDE * 8, 128), f32),
         "unit": vm((1024, 384), f32), "inv_std": vm((1024, 128), f32), "normed": vm((1024, 384), bf16),
@@ -585,6 +586,24 @@
     )(*arrays)
 
 
+def finish_kernel(*refs):
+    for i in range(4):
+        refs[5 + i][...] = refs[i][...]
+    refs[9][0:128] = refs[4][0]
+    refs[9][128:147] = refs[4][1, 0:19]
+
+
+def finish(*arrays):
+    vm = pl.BlockSpec(memory_space=pltpu.VMEM)
+    return pl.pallas_call(
+        finish_kernel,
+        out_shape=tuple(jax.ShapeDtypeStruct(a.shape, a.dtype) for a in arrays[:4]) + (jax.ShapeDtypeStruct((147,), jnp.float32),),
+        in_specs=[vm] * 5,
+        out_specs=(vm,) * 5,
+        name="finish",
+    )(*arrays)
+
+
 def on_device(
     tile_maps,
     positions,
@@ -605,7 +624,7 @@
     slide_bias,
     cotangent,
 ):
-    tile_out, feature, expand_share, reduce_share, depth_share = training_step(
+    results = training_step(
         counts,
         routing,
         positions,
@@ -625,12 +644,13 @@
         slide_bias,
         cotangent,
     )
+    tile_out, feature, expand_share, reduce_share, depth_share = finish(*results)
     return (
         tile_out.reshape((PROC,) + tile_maps.shape[1:]),
         feature,
         expand_share.reshape(-1),
         reduce_share.reshape(-1),
-        depth_share[:2].reshape(-1)[:147],
+        depth_share,
     )
 
 

time: 87.8 us -> 83.6 us (0.952)
  local copies, waits for them, and re-layouts: 5.14 us -> 0 us
  Pallas kernels: 81.1 us -> 82.2 us
    unnamed x10 -> x0, local copies, waits for them, and re-layouts: 3.9 us -> none
    pallas_call x0 -> x1, Pallas kernels: none -> 2.12 us  [finish(): pl.pallas_call(finish_kernel, out_shape=tuple((jax.ShapeDtypeStruct(a.sha...]
    reshape x1 -> x0, local copies, waits for them, and re-layouts: 1.24 us -> none  [on_device(): depth_share[:2].reshape(-1)[:147]]
    pallas_call x1, Pallas kernels: 81.1 us -> 80.1 us  [training_step(): pl.pallas_call(functools.partial(step_kernel, tuple(scratch)), out_shape=...]
where the time goes in v4:
time: 83.6 us; the launch traced here: 83.5 us
  Pallas kernels  82.2 us (98%)
  between operations  1.29 us (2%)
    pallas_call x1, Pallas kernels, training_step(): pl.pallas_call(functools.partial(step_kernel, tuple(scratch)), out_shape=...  80.1 us
    pallas_call x1, Pallas kernels, finish(): pl.pallas_call(finish_kernel, out_shape=tuple((jax.ShapeDtypeStruct(a.sha...  2.12 us

profile of v4, /device:TPU:1, one launch (start us, length us, event | category | flops | bytes accessed | tf_op | source)
XLA Modules:
  0.0 83.5 jit_solution(6733313464726267535)
XLA Ops:
  1.3 80.1 %training_step.1 = (bf16[4,256,384]{2,1,0:T(8,128)(2,1)}, f32[1,768]{1,0:T(1,128)}, f32[36,128]{1,0:T(8,128)}, f32[36,128]{1,0:T(8,128)}, f32[8,128]{1,0:T(8,128)}) custom-call(s32[1]{0:T(128)S(6)} %copy.23.refs_0_, s32[8,1,8]{2,1,0:T(1,128)} %refs_1_.1, s32[2,8]{1,0:T(2,128)} %refs_2_.1, bf16[8,256,384]{2,1,0:T(8,128)(2,1)} %bitcast.4, f32[49,384]{1,0:T(8,128)} %refs_4_.1, ...), custom_call_target="tpu_custom_call" | custom-call | tf_op jit(solution)/shard_map/training_step/pallas_call | solution.py:576
  81.3 2.1 %finish.1 = (bf16[4,256,384]{2,1,0:T(8,128)(2,1)}, f32[1,768]{1,0:T(1,128)}, f32[36,128]{1,0:T(8,128)}, f32[36,128]{1,0:T(8,128)}, f32[147]{0:T(256)}) custom-call(bf16[4,256,384]{2,1,0:T(8,128)(2,1)} %get-tuple-element.15.refs_0_, f32[1,768]{1,0:T(1,128)} %get-tuple-element.16.refs_1_, f32[36,128]{1,0:T(8,128)} %get-tuple-element.17.refs_2_, ...), custom_call_target="tpu_custom_call" | custom-call | tf_op jit(solution)/shard_map/finish/pallas_call | solution.py:598

commit v5 on v4

--- a/solution.py
+++ b/solution.py
@@ -187,12 +187,19 @@
     return departed
 
 
+def far_first(group):
+    x, z = lax.div(group, 4), lax.rem(group, 4)
+    moves = [(i, j) for i in range(4) for j in range(4) if i or j]
+    moves.sort(key=lambda move: -sum(min(step, 4 - step) for step in move))
+    return [lax.rem(x + i, 4) * 4 + lax.rem(z + j, 4) for i, j in moves]
+
+
 def slide_pass(ref, dp, group):
     routing, emb_all, rows_mine, rows_all = ref.routing, ref.emb_all, ref.rows_mine, ref.rows_all
     wide, grad_wide, grad_mine, grad_all = ref.wide, ref.grad_wide, ref.grad_mine, ref.grad_all
     f32, bf16, i32 = jnp.float32, jnp.bfloat16, jnp.int32
     dp_peers = [lax.rem(dp + k, 8) for k in range(1, 8)]
-    group_peers = [lax.rem(group + k, 16) for k in range(1, 16)]
+    group_peers = far_first(group)
 
     def over_dp(source, landing, send, recv):
         copies = []
@@ -378,8 +385,7 @@
     for k in range(7):
         total = total + ref.tap_arrived[k].astype(f32)
     ref.tap_mine[...] = total.astype(bf16)
-    for k in range(1, 16):
-        to = lax.rem(group + k, 16)
+    for k, to in enumerate(far_first(group), 1):
         cp = pltpu.make_async_remote_copy(src_ref=ref.tap_mine, dst_ref=ref.tap_group.at[k - 1], send_sem=ref.tap_send.at[6 + k], recv_sem=ref.tap_recv.at[6 + k], device_id=(dp, to), device_id_type=MESH)
         cp.start()
         copies.append(cp)

time: 83.6 us -> 83 us (level)
  no operation moved by 1% of the time
where the time goes in v5:
time: 83 us; the launch traced here: 82.9 us
  Pallas kernels  81.6 us (98%)
  between operations  1.29 us (2%)
    pallas_call x1, Pallas kernels, training_step(): pl.pallas_call(functools.partial(step_kernel, tuple(scratch)), out_shape=...  79.4 us
    pallas_call x1, Pallas kernels, finish(): pl.pallas_call(finish_kernel, out_shape=tuple((jax.ShapeDtypeStruct(a.sha...  2.12 us

profile of v5, /device:TPU:1, one launch (start us, length us, event | category | flops | bytes accessed | tf_op | source)
XLA Modules:
  0.0 82.9 jit_solution(14017391682458934104)
XLA Ops:
  1.3 79.4 %training_step.1 = (bf16[4,256,384]{2,1,0:T(8,128)(2,1)}, f32[1,768]{1,0:T(1,128)}, f32[36,128]{1,0:T(8,128)}, f32[36,128]{1,0:T(8,128)}, f32[8,128]{1,0:T(8,128)}) custom-call(s32[1]{0:T(128)S(6)} %copy.23.refs_0_, s32[8,1,8]{2,1,0:T(1,128)} %refs_1_.1, s32[2,8]{1,0:T(2,128)} %refs_2_.1, bf16[8,256,384]{2,1,0:T(8,128)(2,1)} %bitcast.4, f32[49,384]{1,0:T(8,128)} %refs_4_.1, ...), custom_call_target="tpu_custom_call" | custom-call | tf_op jit(solution)/shard_map/training_step/pallas_call | solution.py:582
  80.7 2.1 %finish.1 = (bf16[4,256,384]{2,1,0:T(8,128)(2,1)}, f32[1,768]{1,0:T(1,128)}, f32[36,128]{1,0:T(8,128)}, f32[36,128]{1,0:T(8,128)}, f32[147]{0:T(256)}) custom-call(bf16[4,256,384]{2,1,0:T(8,128)(2,1)} %get-tuple-element.15.refs_0_, f32[1,768]{1,0:T(1,128)} %get-tuple-element.16.refs_1_, f32[36,128]{1,0:T(8,128)} %get-tuple-element.17.refs_2_, ...), custom_call_target="tpu_custom_call" | custom-call | tf_op jit(solution)/shard_map/finish/pallas_call | solution.py:604
